TPU v7x, 512 devices: a whole 4x8x8 slice. The times are simulated.
512 devices in a mesh: wide: 32 (over z, x_lo, core), narrow: 16 (over y, x_hi).
Axes of the slice: x: 4 (x_hi: 2, x_lo: 2; x = x_hi * 2 + x_lo), y: 8, z: 8, core: 2. Of those that a mesh axis runs over, the one named last changes fastest.
Arguments:
- left_blocks: bfloat16 [32, 16, 24, 4096], P('wide', 'narrow'), may hold values from -0.59765625 to 0.59765625
- right_blocks: bfloat16 [32, 16, 16, 4096], P('wide', 'narrow'), may hold values from -0.75 to 0.75
- earlier: float32 [32, 16, 16, 4096], P('wide', 'narrow'), may hold values from -6 to 6
- current: float32 [32, 16, 16, 4096], P('wide', 'narrow'), may hold values from -6 to 6
- stack_left: int32 [32, 16, 4, 128], P('wide', 'narrow'), may hold values from 0 to 23
- stack_right: int32 [32, 16, 4, 128], P('wide', 'narrow'), may hold values from 0 to 15
- stack_result: int32 [32, 16, 4, 128], P('wide', 'narrow'), may hold values from 0 to 15
- stack_count: int32 [32, 16, 4], P('wide', 'narrow'), may hold values from 21 to 128, as said below
- keep: int32 [32, 16, 16], P('wide', 'narrow'), may hold values 0 or 1
- send_list: int32 [32, 16, 32, 1], P('wide', 'narrow'), may hold values from 0 to 15
Outputs:
- received: bfloat16 [32, 16, 32, 4096], P('wide', 'narrow')
Inputs may be any that keep to these rules, and one draw needn't show every extreme that they name: `stack_count`: every device has at least 21 live slots in each shift, and some device in every draw has all 128.
All inputs are finite; a program needn't handle non-finite values. No bound on the sum of `keep` on one device may be relied on, other than what follows from the above.
Results may differ from a plain program's by a relative error of at most 0.001.
Values may be sent and summed in bfloat16 or wider, within the bound.
A program may use at most 64 MiB of HBM per device.

v0:
```python
import jax
import jax.numpy as jnp
from jax import lax
from jax.sharding import PartitionSpec as P


def from_behind(value, axis, steps):
    count = lax.axis_size(axis)
    pairs = [(source, (source + steps) % count) for source in range(count)]
    return lax.ppermute(value, axis, pairs)


def stack_products(left, right, sl, sr, sc, count, slots_all, blocks_out):
    edge = 64
    group = min(256, slots_all)
    left_mat = left.reshape(left.shape[0], edge, edge)
    right_mat = right.reshape(right.shape[0], edge, edge)
    targets = jnp.arange(blocks_out, dtype=jnp.int32)

    def add_group(g, acc):
        start = g * group
        prod = jnp.einsum(
            "gij,gjk->gik", left_mat[sl], right_mat[sr], preferred_element_type=jnp.float32
        )
        slots = start + jnp.arange(group, dtype=jnp.int32)
        live = slots < count
        table = ((targets[:, None] == sc[None, :]) & live[None, :]).astype(jnp.float32)
        return acc + jnp.dot(
            table,
            prod.reshape(group, edge * edge),
            precision=lax.Precision.HIGHEST,
            preferred_element_type=jnp.float32,
        )

    empty = jnp.zeros((blocks_out, edge * edge), jnp.float32)
    return lax.fori_loop(0, slots_all // group, add_group, empty)


def per_device(
    left_blocks,
    right_blocks,
    earlier,
    current,
    stack_left,
    stack_right,
    stack_result,
    stack_count,
    keep,
    send_list,
):
    blocks_out = earlier.shape[2]
    slots_all = stack_left.shape[3]
    shift_total = stack_left.shape[2]
    left_start = left_blocks[0, 0]
    right_start = right_blocks[0, 0]
    total = earlier[0, 0]
    left_now = left_start
    right_now = right_start
    for shift in range(shift_total):
        if shift > 0:
            left_now = from_behind(left_now, "wide", -1)
            right_now = from_behind(right_now, "narrow", -1)
        total = total + stack_products(
            left_now,
            right_now,
            stack_left[0, 0, shift],
            stack_right[0, 0, shift],
            stack_result[0, 0, shift],
            stack_count[0, 0, shift],
            slots_all,
            blocks_out,
        )
    updated = (
        (1.5 * current[0, 0] - 0.5 * total) * keep[0, 0].astype(jnp.float32)[:, None]
    ).astype(jnp.bfloat16)
    outgoing = updated[send_list[0, 0]]
    arrived = lax.all_to_all(outgoing, "wide", split_axis=0, concat_axis=0, tiled=True)
    owners = arrived.shape[0] * arrived.shape[1]
    return arrived.reshape(1, 1, owners, arrived.shape[2])


def solution(mesh):
    placed = (
        P("wide", "narrow", None, None),
        P("wide", "narrow", None, None),
        P("wide", "narrow", None, None),
        P("wide", "narrow", None, None),
        P("wide", "narrow", None, None),
        P("wide", "narrow", None, None),
        P("wide", "narrow", None, None),
        P("wide", "narrow", None),
        P("wide", "narrow", None),
        P("wide", "narrow", None, None),
    )
    return jax.shard_map(
        per_device,
        mesh=mesh,
        in_specs=placed,
        out_specs=P("wide", "narrow", None, None),
        check_vma=False,
    )
```

profile of v0, /device:TPU:1, one launch (start us, length us, event | category | flops | bytes accessed | tf_op | source)
XLA Modules:
  0.0 121.3 jit_solution(8204672547003219371)
XLA Ops:
  0.0 8.8 %collective-permute-start = (bf16[24,4096]{1,0:T(8,128)(2,1)}, bf16[24,4096]{1,0:T(8,128)(2,1)S(1)}, u32[]{:S(2)}, u32[]{:S(2)}) collective-permute-start(bf16[24,4096]{1,0:T(8,128)(2,1)} %bitcast.85), channel_id=1, source_target_pairs={{0,496},{16,0},{32,16},{48,32},{64,48},{80,64},{96,80},{112,96},{1... | collective-permute-start | bytes 589832 | tf_op jit(solution)/shard_map/ppermute | solution.py:10
  8.8 2.2 %collective-permute-start.1 = (bf16[16,4096]{1,0:T(8,128)(2,1)}, bf16[16,4096]{1,0:T(8,128)(2,1)S(1)}, u32[]{:S(2)}, u32[]{:S(2)}) collective-permute-start(bf16[16,4096]{1,0:T(8,128)(2,1)} %bitcast.86), channel_id=1, source_target_pairs={{0,15},{1,0},{2,1},{3,2},{4,3},{5,4},{6,5},{7,6},{8,7},{9,8},{10,9... | collective-permute-start | bytes 393224 | tf_op jit(solution)/shard_map/ppermute | solution.py:10
  11.0 1.3 %reshape_squeeze.6 = bf16[24,64,64]{2,1,0:T(8,128)(2,1)S(1)} reshape(bf16[1,1,24,4096]{3,2,1,0:T(8,128)(2,1)} %param.10) | data formatting | bytes 393216 | tf_op jit(solution)/shard_map/reshape;squeeze | solution.py:16
  12.3 1.2 reshape_squeeze.7
  16.1 2.2 %gather_fusion.1 = bf16[128,64,64]{2,1,0:T(8,128)(2,1)} fusion(bf16[16,64,64]{2,1,0:T(8,128)(2,1)S(1)} %reshape_squeeze.7, s32[1024]{0:T(1024)S(1)} %pad_clamp_fusion.7), kind=kCustom, calls=%fused_computation.1 | custom fusion | bytes 2097664 | tf_op jit(solution)/shard_map/while/body/eval_jaxpr/gather | solution.py:23
  18.3 4.2 %fusion.30 = f32[128,64,64]{2,1,0:T(8,128)} fusion(bf16[128,64,64]{2,1,0:T(8,128)(2,1)S(1)} %gather_fusion, bf16[128,64,64]{2,1,0:T(8,128)(2,1)} %gather_fusion.1), kind=kOutput, calls=%fused_computation.71 | convolution fusion | flops 67108864 | bytes 4194304 | tf_op jit(solution)/shard_map/while/body/eval_jaxpr/gij,gjk->gik/dot_general | solution.py:22
  22.6 3.9 %copy.20 = f32[128,64,64]{0,2,1:T(8,128)S(1)} copy(f32[128,64,64]{2,1,0:T(8,128)} %fusion.30) | data formatting | bytes 4194304 | tf_op jit(solution)/shard_map/while/body/eval_jaxpr/gij,gjk->gik/dot_general | solution.py:22
  28.4 1.2 %iota_compare_fusion.6 = pred[128]{0:T(512)(128)(4,1)} fusion(s32[]{:T(128)} %bitcast.10), kind=kLoop, calls=%fused_computation.66 | loop fusion | flops 128 | bytes 132 | tf_op jit(solution)/shard_map/while/body/eval_jaxpr/lt | solution.py:26
  30.2 1.1 iota_compare_fusion.5
  31.9 1.1 convolution_add_fusion.3
  32.9 1.2 %iota_compare_fusion.4 = pred[128]{0:T(512)(128)(4,1)} fusion(s32[]{:T(128)} %bitcast.26), kind=kLoop, calls=%fused_computation.62 | loop fusion | flops 128 | bytes 132 | tf_op jit(solution)/shard_map/while/body/eval_jaxpr/lt | solution.py:26
  35.4 2.1 %collective-permute-start.3 = (bf16[16,4096]{1,0:T(8,128)(2,1)S(1)}, bf16[16,4096]{1,0:T(8,128)(2,1)S(1)}, u32[]{:S(2)}, u32[]{:S(2)}) collective-permute-start(bf16[16,4096]{1,0:T(8,128)(2,1)S(1)} %collective-permute-done.1), channel_id=1, source_target_pairs={{0,15},{1,0},{2,1},{3,2},{4,3},{5,4},{6,5},{7,6},{8,7},{9,8},{10,9... | collective-permute-start | bytes 393224 | tf_op jit(solution)/shard_map/ppermute | solution.py:10
  37.9 2.2 %gather_fusion.2 = bf16[128,64,64]{2,1,0:T(8,128)(2,1)} fusion(bf16[24,64,64]{2,1,0:T(8,128)(2,1)S(1)} %reshape.329, s32[1024]{0:T(1024)S(1)} %pad_clamp_fusion.6), kind=kCustom, calls=%fused_computation.2 | custom fusion | bytes 2097664 | tf_op jit(solution)/shard_map/while/body/eval_jaxpr/gather | solution.py:23
  40.1 4.2 %fusion.31 = f32[128,64,64]{2,1,0:T(8,128)} fusion(bf16[128,64,64]{2,1,0:T(8,128)(2,1)} %gather_fusion.2, bf16[128,64,64]{2,1,0:T(8,128)(2,1)S(1)} %gather_fusion.3), kind=kOutput, calls=%fused_computation.72 | convolution fusion | flops 67108864 | bytes 4194304 | tf_op jit(solution)/shard_map/while/body/eval_jaxpr/gij,gjk->gik/dot_general | solution.py:22
  44.3 3.8 %copy.21 = f32[128,64,64]{0,2,1:T(8,128)S(1)} copy(f32[128,64,64]{2,1,0:T(8,128)} %fusion.31) | data formatting | bytes 4194304 | tf_op jit(solution)/shard_map/while/body/eval_jaxpr/gij,gjk->gik/dot_general | solution.py:22
  48.1 11.9 %collective-permute-start.2 = (bf16[24,4096]{1,0:T(8,128)(2,1)S(1)}, bf16[24,4096]{1,0:T(8,128)(2,1)S(1)}, u32[]{:S(2)}, u32[]{:S(2)}) collective-permute-start(bf16[24,4096]{1,0:T(8,128)(2,1)S(1)} %collective-permute-done), channel_id=1, source_target_pairs={{0,496},{16,0},{32,16},{48,32},{64,48},{80,64},{96,80},{112,96},{1... | collective-permute-start | bytes 589832 | tf_op jit(solution)/shard_map/ppermute | solution.py:10
  60.0 5.4 %collective-permute-start.5 = (bf16[16,4096]{1,0:T(8,128)(2,1)S(1)}, bf16[16,4096]{1,0:T(8,128)(2,1)}, u32[]{:S(2)}, u32[]{:S(2)}) collective-permute-start(bf16[16,4096]{1,0:T(8,128)(2,1)S(1)} %collective-permute-done.3), channel_id=1, source_target_pairs={{0,15},{1,0},{2,1},{3,2},{4,3},{5,4},{6,5},{7,6},{8,7},{9,8},{10,9... | collective-permute-start | bytes 393224 | tf_op jit(solution)/shard_map/ppermute | solution.py:10
  65.4 1.1 convolution_add_fusion.2
  66.7 1.1 gather_fusion.5
  68.6 1.2 reshape.336
  69.8 2.2 %gather_fusion.7 = bf16[128,64,64]{2,1,0:T(8,128)(2,1)} fusion(bf16[16,64,64]{2,1,0:T(8,128)(2,1)S(1)} %reshape.336, s32[1024]{0:T(1024)S(1)} %pad_clamp_fusion.1), kind=kCustom, calls=%fused_computation.7 | custom fusion | bytes 2097664 | tf_op jit(solution)/shard_map/while/body/eval_jaxpr/gather | solution.py:23
  72.3 2.2 %gather_fusion.4 = bf16[128,64,64]{2,1,0:T(8,128)(2,1)} fusion(bf16[24,64,64]{2,1,0:T(8,128)(2,1)S(1)} %reshape.332, s32[1024]{0:T(1024)S(1)} %pad_clamp_fusion.4), kind=kCustom, calls=%fused_computation.4 | custom fusion | bytes 2097664 | tf_op jit(solution)/shard_map/while/body/eval_jaxpr/gather | solution.py:23
  74.5 4.2 %fusion.32 = f32[128,64,64]{2,1,0:T(8,128)} fusion(bf16[128,64,64]{2,1,0:T(8,128)(2,1)} %gather_fusion.4, bf16[128,64,64]{2,1,0:T(8,128)(2,1)S(1)} %gather_fusion.5), kind=kOutput, calls=%fused_computation.73 | convolution fusion | flops 67108864 | bytes 4194304 | tf_op jit(solution)/shard_map/while/body/eval_jaxpr/gij,gjk->gik/dot_general | solution.py:22
  78.7 3.8 %copy.22 = f32[128,64,64]{0,2,1:T(8,128)S(1)} copy(f32[128,64,64]{2,1,0:T(8,128)} %fusion.32) | data formatting | bytes 4194304 | tf_op jit(solution)/shard_map/while/body/eval_jaxpr/gij,gjk->gik/dot_general | solution.py:22
  82.5 2.8 %collective-permute-start.4 = (bf16[24,4096]{1,0:T(8,128)(2,1)S(1)}, bf16[24,4096]{1,0:T(8,128)(2,1)S(1)}, u32[]{:S(2)}, u32[]{:S(2)}) collective-permute-start(bf16[24,4096]{1,0:T(8,128)(2,1)S(1)} %collective-permute-done.2), channel_id=1, source_target_pairs={{0,496},{16,0},{32,16},{48,32},{64,48},{80,64},{96,80},{112,96},{1... | collective-permute-start | bytes 589832 | tf_op jit(solution)/shard_map/ppermute | solution.py:10
  85.4 1.1 convolution_add_fusion.1
  86.4 3.1 %collective-permute-done.4 = bf16[24,4096]{1,0:T(8,128)(2,1)S(1)} collective-permute-done((bf16[24,4096]{1,0:T(8,128)(2,1)S(1)}, bf16[24,4096]{1,0:T(8,128)(2,1)S(1)}, u32[]{:S(2)}, u32[]{:S(2)}) %collective-permute-start.4) | collective-permute-done | bytes 196640 | tf_op jit(solution)/shard_map/ppermute | solution.py:10
  89.9 2.2 %gather_fusion.6 = bf16[128,64,64]{2,1,0:T(8,128)(2,1)} fusion(bf16[24,64,64]{2,1,0:T(8,128)(2,1)S(1)} %reshape.335, s32[1024]{0:T(1024)S(1)} %pad_clamp_fusion.2), kind=kCustom, calls=%fused_computation.6 | custom fusion | bytes 2097664 | tf_op jit(solution)/shard_map/while/body/eval_jaxpr/gather | solution.py:23
  92.1 4.2 %fusion.33 = f32[128,64,64]{2,1,0:T(8,128)} fusion(bf16[128,64,64]{2,1,0:T(8,128)(2,1)} %gather_fusion.6, bf16[128,64,64]{2,1,0:T(8,128)(2,1)S(1)} %copy-done), kind=kOutput, calls=%fused_computation.74 | convolution fusion | flops 67108864 | bytes 4194304 | tf_op jit(solution)/shard_map/while/body/eval_jaxpr/gij,gjk->gik/dot_general | solution.py:22
  96.3 3.8 %copy.23 = f32[128,64,64]{0,2,1:T(8,128)S(1)} copy(f32[128,64,64]{2,1,0:T(8,128)} %fusion.33) | data formatting | bytes 4194304 | tf_op jit(solution)/shard_map/while/body/eval_jaxpr/gij,gjk->gik/dot_general | solution.py:22
  100.2 1.1 fusion.3
  103.5 16.5 %all_to_all.5 = bf16[32,2,2048]{2,1,0:T(2,128)(2,1)S(1)} all-to-all(bf16[32,2,2048]{2,1,0:T(2,128)(2,1)S(1)} %reshape.411), channel_id=1, replica_groups=mesh['wide'=32,'narrow'=16] {'wide'}, dimensions={0} | all-to-all | bytes 524288 | tf_op jit(solution)/shard_map/all_to_all | solution.py:77
  (62 shorter events, 12.5 us)
Async XLA Ops:
  0.0 37.5 %collective-permute-start = (bf16[24,4096]{1,0:T(8,128)(2,1)}, bf16[24,4096]{1,0:T(8,128)(2,1)S(1)}, u32[]{:S(2)}, u32[]{:S(2)}) collective-permute-start(bf16[24,4096]{1,0:T(8,128)(2,1)} %bitcast.85), channel_id=1, source_target_pairs={{0,496},{16,0},{32,16},{48,32},{64,48},{80,64},{96,80},{112,96},{1... | collective-permute-start | bytes 589832 | tf_op jit(solution)/shard_map/ppermute | solution.py:10
  8.8 25.4 %collective-permute-start.1 = (bf16[16,4096]{1,0:T(8,128)(2,1)}, bf16[16,4096]{1,0:T(8,128)(2,1)S(1)}, u32[]{:S(2)}, u32[]{:S(2)}) collective-permute-start(bf16[16,4096]{1,0:T(8,128)(2,1)} %bitcast.86), channel_id=1, source_target_pairs={{0,15},{1,0},{2,1},{3,2},{4,3},{5,4},{6,5},{7,6},{8,7},{9,8},{10,9... | collective-permute-start | bytes 393224 | tf_op jit(solution)/shard_map/ppermute | solution.py:10
  22.5 3.9 %copy-start.3 = (s32[1,1,4]{2,1,0:T(1,128)S(1)}, s32[1,1,4]{2,1,0:T(1,128)}, u32[]{:S(2)}) copy-start(s32[1,1,4]{2,1,0:T(1,128)} %param.17) | copy-start | bytes 52
  22.5 5.2 %copy-start.6 = (s32[1,1,4,128]{3,2,1,0:T(4,128)S(1)}, s32[1,1,4,128]{3,2,1,0:T(4,128)}, u32[]{:S(2)}) copy-start(s32[1,1,4,128]{3,2,1,0:T(4,128)} %param.16) | copy-start | bytes 6148
  22.5 8.8 %copy-start.12 = (s32[1,1,16]{2,1,0:T(1,128)S(1)}, s32[1,1,16]{2,1,0:T(1,128)}, u32[]{:S(2)}) copy-start(s32[1,1,16]{2,1,0:T(1,128)} %param.18) | copy-start | bytes 196
  22.5 9.3 %copy-start.13 = (s32[1,1,32,1]{2,3,1,0:T(1,128)S(1)}, s32[1,1,32,1]{2,3,1,0:T(1,128)}, u32[]{:S(2)}) copy-start(s32[1,1,32,1]{2,3,1,0:T(1,128)} %param.19) | copy-start | bytes 388
  22.5 9.3 %copy-start.1 = (f32[1,1,16,4096]{3,2,1,0:T(8,128)S(1)}, f32[1,1,16,4096]{3,2,1,0:T(8,128)}, u32[]{:S(2)}) copy-start(f32[1,1,16,4096]{3,2,1,0:T(8,128)} %param.12) | copy-start | bytes 786436
  35.4 24.6 %collective-permute-start.3 = (bf16[16,4096]{1,0:T(8,128)(2,1)S(1)}, bf16[16,4096]{1,0:T(8,128)(2,1)S(1)}, u32[]{:S(2)}, u32[]{:S(2)}) collective-permute-start(bf16[16,4096]{1,0:T(8,128)(2,1)S(1)} %collective-permute-done.1), channel_id=1, source_target_pairs={{0,15},{1,0},{2,1},{3,2},{4,3},{5,4},{6,5},{7,6},{8,7},{9,8},{10,9... | collective-permute-start | bytes 393224 | tf_op jit(solution)/shard_map/ppermute | solution.py:10
  44.3 21.1 %copy-start.5 = (s32[128]{0:T(128)S(1)}, s32[128]{0:T(128)}, u32[]{:S(2)}) copy-start(s32[128]{0:T(128)} %get-tuple-element.84) | copy-start | bytes 1540
  44.3 21.1 %copy-start.9 = (pred[128]{0:T(512)(128)(4,1)S(1)}, pred[128]{0:T(512)(128)(4,1)}, u32[]{:S(2)}) copy-start(pred[128]{0:T(512)(128)(4,1)} %iota_compare_fusion.6) | copy-start | bytes 388
  48.1 23.8 %collective-permute-start.2 = (bf16[24,4096]{1,0:T(8,128)(2,1)S(1)}, bf16[24,4096]{1,0:T(8,128)(2,1)S(1)}, u32[]{:S(2)}, u32[]{:S(2)}) collective-permute-start(bf16[24,4096]{1,0:T(8,128)(2,1)S(1)} %collective-permute-done), channel_id=1, source_target_pairs={{0,496},{16,0},{32,16},{48,32},{64,48},{80,64},{96,80},{112,96},{1... | collective-permute-start | bytes 589832 | tf_op jit(solution)/shard_map/ppermute | solution.py:10
  60.0 8.6 %collective-permute-start.5 = (bf16[16,4096]{1,0:T(8,128)(2,1)S(1)}, bf16[16,4096]{1,0:T(8,128)(2,1)}, u32[]{:S(2)}, u32[]{:S(2)}) collective-permute-start(bf16[16,4096]{1,0:T(8,128)(2,1)S(1)} %collective-permute-done.3), channel_id=1, source_target_pairs={{0,15},{1,0},{2,1},{3,2},{4,3},{5,4},{6,5},{7,6},{8,7},{9,8},{10,9... | collective-permute-start | bytes 393224 | tf_op jit(solution)/shard_map/ppermute | solution.py:10
  78.7 6.6 %copy-start.4 = (s32[128]{0:T(128)S(1)}, s32[128]{0:T(128)}, u32[]{:S(2)}) copy-start(s32[128]{0:T(128)} %get-tuple-element.86) | copy-start | bytes 1540
  78.7 6.6 %copy-start.8 = (pred[128]{0:T(512)(128)(4,1)S(1)}, pred[128]{0:T(512)(128)(4,1)}, u32[]{:S(2)}) copy-start(pred[128]{0:T(512)(128)(4,1)} %iota_compare_fusion.5) | copy-start | bytes 388
  82.5 7.0 %collective-permute-start.4 = (bf16[24,4096]{1,0:T(8,128)(2,1)S(1)}, bf16[24,4096]{1,0:T(8,128)(2,1)S(1)}, u32[]{:S(2)}, u32[]{:S(2)}) collective-permute-start(bf16[24,4096]{1,0:T(8,128)(2,1)S(1)} %collective-permute-done.2), channel_id=1, source_target_pairs={{0,496},{16,0},{32,16},{48,32},{64,48},{80,64},{96,80},{112,96},{1... | collective-permute-start | bytes 589832 | tf_op jit(solution)/shard_map/ppermute | solution.py:10
  89.9 2.2 %copy-start = (bf16[128,64,64]{2,1,0:T(8,128)(2,1)S(1)}, bf16[128,64,64]{2,1,0:T(8,128)(2,1)}, u32[]{:S(2)}) copy-start(bf16[128,64,64]{2,1,0:T(8,128)(2,1)} %gather_fusion.7) | copy-start | bytes 3145732
  96.3 3.9 %copy-start.2 = (f32[1,1,16,4096]{3,2,1,0:T(8,128)S(1)}, f32[1,1,16,4096]{3,2,1,0:T(8,128)}, u32[]{:S(2)}) copy-start(f32[1,1,16,4096]{3,2,1,0:T(8,128)} %param.13) | copy-start | bytes 786436
  96.3 3.9 %copy-start.7 = (s32[128]{0:T(128)S(1)}, s32[128]{0:T(128)}, u32[]{:S(2)}) copy-start(s32[128]{0:T(128)} %get-tuple-element.83) | copy-start | bytes 1540
  96.3 3.9 %copy-start.10 = (f32[16]{0:T(128)S(1)}, f32[16]{0:T(128)}, u32[]{:S(2)}) copy-start(f32[16]{0:T(128)} %convert_bitcast_fusion) | copy-start | bytes 196
  96.3 3.9 %copy-start.11 = (pred[128]{0:T(512)(128)(4,1)S(1)}, pred[128]{0:T(512)(128)(4,1)}, u32[]{:S(2)}) copy-start(pred[128]{0:T(512)(128)(4,1)} %iota_compare_fusion.4) | copy-start | bytes 388
where the time goes:
time: 122 us; the launch traced here: 121 us
  local copies, waits for them, and re-layouts  38.4 us (31%)
  starting transfers between devices  33.1 us (27%)
  matrix products  21.1 us (17%)
  blocking collectives  16.5 us (14%)
  other arithmetic  7.85 us (6%)
  waiting for transfers between devices  3.93 us (3%)
    ppermute x6, starting transfers between devices, from_behind(): return lax.ppermute(value, axis, pairs)  33.1 us
    dot_general x4, matrix products, add_group(): jnp.einsum('gij,gjk->gik', left_mat[sl], right_mat[sr], preferred_element...  16.9 us
    all_to_all x1, blocking collectives, per_device(): lax.all_to_all(outgoing, 'wide', split_axis=0, concat_axis=0, tiled=True)  16.5 us
    dot_general x4, local copies, waits for them, and re-layouts, add_group(): jnp.einsum('gij,gjk->gik', left_mat[sl], right_mat[sr], preferred_element...  15.3 us
    gather x4, local copies, waits for them, and re-layouts, add_group(): left_mat[sl]  7.49 us
    gather x4, local copies, waits for them, and re-layouts, add_group(): right_mat[sr]  6.37 us
    lt x4, other arithmetic, add_group(): live = slots < count  4.24 us
    dot_general x4, matrix products, add_group(): jnp.dot(table, prod.reshape(group, edge * edge), precision=lax.Precision....  4.23 us
  transfers between devices with their start and end apart: 6, of which 2 were waited for; matrix products, arithmetic and copies ran while one was open for 34% of the time, Pallas kernels for 0%

commit v1 on v0

v1 whole, which is shorter than its diff:
```python
import functools

import jax
import jax.numpy as jnp
from jax import lax
from jax.experimental import pallas as pl
from jax.experimental.pallas import tpu as pltpu
from jax.sharding import PartitionSpec as P

MESH = pl.DeviceIdType.MESH
EDGE = 64
LANES = 128


def kernel(
    n_wide,
    n_narrow,
    shifts,
    l_ref,
    r_ref,
    e_ref,
    c_ref,
    sl_ref,
    sr_ref,
    sc_ref,
    cnt_ref,
    keep_ref,
    send_ref,
    out_ref,
    lbuf,
    rbuf,
    ebuf,
    cbuf,
    rq,
    rd,
    wsel,
    ahi,
    alo,
    wt,
    tot,
    upd,
    rows,
    outgoing,
    lsend,
    lrecv,
    rsend,
    rrecv,
    esem,
    asend,
    arecv,
):
    w = lax.axis_index("wide")
    n = lax.axis_index("narrow")
    nl = l_ref.shape[0]
    nr = r_ref.shape[0]
    nc = e_ref.shape[0]
    tiles = l_ref.shape[1] // LANES
    bf16, f32 = jnp.bfloat16, jnp.float32

    own_l = pltpu.make_async_copy(l_ref, lbuf.at[0], lrecv.at[0])
    own_l.start()
    get_e = pltpu.make_async_copy(e_ref, ebuf, esem.at[0])
    get_e.start()
    get_c = pltpu.make_async_copy(c_ref, cbuf, esem.at[1])
    get_c.start()

    barrier = pltpu.get_barrier_semaphore()

    def greet(k, carry):
        pl.semaphore_signal(
            barrier, inc=1, device_id={"wide": lax.rem(w + k, n_wide)}, device_id_type=MESH
        )
        return carry

    lax.fori_loop(1, n_wide, greet, 0)
    for k in range(1, shifts):
        for other in (n + k, n + n_narrow - k):
            pl.semaphore_signal(
                barrier, inc=1, device_id={"narrow": lax.rem(other, n_narrow)}, device_id_type=MESH
            )
    pl.semaphore_wait(barrier, n_wide - 1 + 2 * (shifts - 1))

    l_copies = []
    for k in range(1, shifts):
        copy = pltpu.make_async_remote_copy(
            src_ref=l_ref,
            dst_ref=lbuf.at[k],
            send_sem=lsend.at[k],
            recv_sem=lrecv.at[k],
            device_id={"wide": lax.rem(w + n_wide - k, n_wide)},
            device_id_type=MESH,
        )
        copy.start()
        l_copies.append(copy)

    lane = lax.broadcasted_iota(jnp.int32, (EDGE // 2, LANES), 1)
    low = lane < EDGE
    for t in range(tiles):
        rq[pl.ds(t, nr, stride=tiles), :] = r_ref[:, t * LANES : (t + 1) * LANES].astype(f32)
    for p in range(nr // 2):
        even = rq[(2 * p) * tiles : (2 * p + 1) * tiles, :]
        odd = rq[(2 * p + 1) * tiles : (2 * p + 2) * tiles, :]
        rd[pl.ds(p * EDGE, EDGE // 2, stride=2), :] = jnp.where(low, even, pltpu.roll(odd, EDGE, 1))
        rd[pl.ds(p * EDGE + 1, EDGE // 2, stride=2), :] = jnp.where(
            low, pltpu.roll(even, EDGE, 1), odd
        )
    rbuf[0] = rd[...].astype(bf16)

    r_copies = []
    for k in range(1, shifts):
        copy = pltpu.make_async_remote_copy(
            src_ref=rbuf.at[0],
            dst_ref=rbuf.at[k],
            send_sem=rsend.at[k],
            recv_sem=rrecv.at[k],
            device_id={"narrow": lax.rem(n + n_narrow - k, n_narrow)},
            device_id_type=MESH,
        )
        copy.start()
        r_copies.append(copy)

    slots = sl_ref.shape[1]
    slot = lax.broadcasted_iota(jnp.int32, (1, slots), 1)
    for s in range(shifts):
        live = slot < cnt_ref[0, s]
        cell = jnp.where(live, sr_ref[s : s + 1, :] * nc + sc_ref[s : s + 1, :], -1)
        cells = lax.broadcasted_iota(jnp.int32, (nr * nc, slots), 0) == cell
        lefts = lax.broadcasted_iota(jnp.int32, (nl, slots), 0) == sl_ref[s : s + 1, :]
        wsel[s] = lax.dot_general(
            cells.astype(f32).astype(bf16),
            lefts.astype(f32).astype(bf16),
            (((1,), (1,)), ((), ())),
            preferred_element_type=f32,
        ).astype(bf16)

    tot[...] = jnp.zeros_like(tot)
    lane_w = lax.broadcasted_iota(jnp.int32, (EDGE, LANES), 1)
    low_w = lane_w < EDGE

    def one_shift(s, carry):
        @pl.when(s > 0)
        def _():
            pltpu.make_async_copy(rbuf.at[s], rbuf.at[s], rrecv.at[s]).wait()

        def weights(p, carry):
            pair = rbuf[s, pl.ds(pl.multiple_of(p * EDGE, EDGE), EDGE), :].astype(f32)
            turned = pltpu.roll(pair, EDGE, 1)
            base = pl.multiple_of(p * 4 * EDGE, 4 * EDGE)
            wt[pl.ds(base, EDGE), :] = jnp.where(low_w, pair, 0.0).astype(bf16)
            wt[pl.ds(base + EDGE, EDGE), :] = jnp.where(low_w, 0.0, turned).astype(bf16)
            wt[pl.ds(base + 2 * EDGE, EDGE), :] = jnp.where(low_w, turned, 0.0).astype(bf16)
            wt[pl.ds(base + 3 * EDGE, EDGE), :] = jnp.where(low_w, 0.0, pair).astype(bf16)
            return carry

        lax.fori_loop(0, nr // 2, weights, 0)
        pltpu.make_async_copy(lbuf.at[s], lbuf.at[s], lrecv.at[s]).wait()
        sel = wsel[s]

        def spread(q, carry):
            cols = pl.multiple_of(q * 2 * LANES, 2 * LANES)
            a = jnp.dot(sel, lbuf[s, :, pl.ds(cols, 2 * LANES)], preferred_element_type=f32)
            hi = a.astype(bf16)
            lo = (a - hi.astype(f32)).astype(bf16)
            for h in range(2):
                at = pl.ds(pl.multiple_of((2 * q + h) * nc, nc), nc)
                for r in range(nr):
                    src = (slice(r * nc, (r + 1) * nc), slice(h * LANES, (h + 1) * LANES))
                    ahi[at, r * LANES : (r + 1) * LANES] = hi[src]
                    alo[at, r * LANES : (r + 1) * LANES] = lo[src]
            return carry

        lax.fori_loop(0, tiles // 2, spread, 0)

        def multiply(m, carry):
            at = pl.ds(pl.multiple_of(m * 128, 128), 128)
            tot[at, :] += jnp.dot(
                ahi[at, :], wt[...], preferred_element_type=f32
            ) + jnp.dot(alo[at, :], wt[...], preferred_element_type=f32)
            return carry

        lax.fori_loop(0, tiles * nc // 128, multiply, 0)
        return carry

    lax.fori_loop(0, shifts, one_shift, 0)

    get_e.wait()
    get_c.wait()
    eye = lax.broadcasted_iota(jnp.int32, (nc, nc), 0) == lax.broadcasted_iota(jnp.int32, (nc, nc), 1)
    keep = jnp.sum(jnp.where(eye, keep_ref[...].astype(f32), 0.0), axis=1, keepdims=True)
    for t in range(tiles):
        cols = slice(t * LANES, (t + 1) * LANES)
        total = ebuf[:, cols] + tot[t * nc : (t + 1) * nc, :]
        upd[:, cols] = ((1.5 * cbuf[:, cols] - 0.5 * total) * keep).astype(bf16)
    eye_w = lax.broadcasted_iota(jnp.int32, (n_wide, n_wide), 0) == lax.broadcasted_iota(
        jnp.int32, (n_wide, n_wide), 1
    )
    sends = jnp.sum(jnp.where(eye_w, send_ref[...].astype(f32), 0.0), axis=1, keepdims=True)
    pick = (
        (lax.broadcasted_iota(jnp.int32, (n_wide, nc), 1) == sends.astype(jnp.int32))
        .astype(f32)
        .astype(bf16)
    )
    for t in range(0, tiles, 4):
        picked = jnp.dot(pick, upd[:, t * LANES : (t + 4) * LANES], preferred_element_type=f32)
        for h in range(4):
            rows[pl.ds(t + h, n_wide, stride=tiles), :] = picked[:, h * LANES : (h + 1) * LANES]
    for d in range(n_wide):
        outgoing[d] = rows[d * tiles : (d + 1) * tiles, :].astype(bf16)

    keep_own = pltpu.make_async_copy(outgoing.at[w], out_ref.at[w], arecv.at[w])
    keep_own.start()

    def block_copy(k):
        d = lax.rem(w + k, n_wide)
        return pltpu.make_async_remote_copy(
            src_ref=outgoing.at[d],
            dst_ref=out_ref.at[w],
            send_sem=asend.at[d],
            recv_sem=arecv.at[w],
            device_id={"wide": d},
            device_id_type=MESH,
        )

    def send_block(k, carry):
        block_copy(k).start()
        return carry

    lax.fori_loop(1, n_wide, send_block, 0)

    for copy in l_copies:
        copy.wait_send()
    for copy in r_copies:
        copy.wait_send()
    keep_own.wait()

    def settle(k, carry):
        block_copy(k).wait_send()
        src = lax.rem(w + k, n_wide)
        pltpu.make_async_copy(out_ref.at[src], out_ref.at[src], arecv.at[src]).wait()
        return carry

    lax.fori_loop(1, n_wide, settle, 0)


def per_device(n_wide, n_narrow, left, right, earlier, current, sl, sr, sc, count, keep, send):
    left, right, earlier, current = left[0, 0], right[0, 0], earlier[0, 0], current[0, 0]
    sl, sr, sc = sl[0, 0], sr[0, 0], sc[0, 0]
    shifts = sl.shape[0]
    nl, flat = left.shape
    nr = right.shape[0]
    nc = earlier.shape[0]
    tiles = flat // LANES
    count = count.reshape(1, shifts)
    keep = keep.reshape(1, nc)
    send = send.reshape(1, n_wide)
    bf16, f32 = jnp.bfloat16, jnp.float32
    vmem = pl.BlockSpec(memory_space=pltpu.VMEM)
    smem = pl.BlockSpec(memory_space=pltpu.SMEM)
    hbm = pl.BlockSpec(memory_space=pl.ANY)
    dma = pltpu.SemaphoreType.DMA
    out = pl.pallas_call(
        functools.partial(kernel, n_wide, n_narrow, shifts),
        out_shape=jax.ShapeDtypeStruct((n_wide, tiles, LANES), bf16),
        in_specs=[hbm, vmem, hbm, hbm, vmem, vmem, vmem, smem, vmem, vmem],
        out_specs=hbm,
        scratch_shapes=[
            pltpu.VMEM((shifts, nl, flat), bf16),
            pltpu.VMEM((shifts, nr // 2 * EDGE, LANES), bf16),
            pltpu.VMEM((nc, flat), f32),
            pltpu.VMEM((nc, flat), f32),
            pltpu.VMEM((nr * tiles, LANES), f32),
            pltpu.VMEM((nr // 2 * EDGE, LANES), f32),
            pltpu.VMEM((shifts, nr * nc, nl), bf16),
            pltpu.VMEM((tiles * nc, nr * LANES), bf16),
            pltpu.VMEM((tiles * nc, nr * LANES), bf16),
            pltpu.VMEM((nr * LANES, LANES), bf16),
            pltpu.VMEM((tiles * nc, LANES), f32),
            pltpu.VMEM((nc, flat), bf16),
            pltpu.VMEM((n_wide * tiles, LANES), f32),
            pltpu.VMEM((n_wide, tiles, LANES), bf16),
            dma((shifts,)),
            dma((shifts,)),
            dma((shifts,)),
            dma((shifts,)),
            dma((2,)),
            dma((n_wide,)),
            dma((n_wide,)),
        ],
        compiler_params=pltpu.CompilerParams(
            collective_id=0, has_side_effects=True, vmem_limit_bytes=40 * 1024 * 1024
        ),
        cost_estimate=pl.CostEstimate(
            flops=2 * shifts * 4096 * 256 * 256 * 3, bytes_accessed=4 << 20, transcendentals=0
        ),
    )(left, right, earlier, current, sl, sr, sc, count, keep, send)
    return out.reshape(1, 1, n_wide, flat)


def solution(mesh):
    spec4 = P("wide", "narrow", None, None)
    spec3 = P("wide", "narrow", None)
    return jax.shard_map(
        functools.partial(per_device, mesh.shape["wide"], mesh.shape["narrow"]),
        mesh=mesh,
        in_specs=(spec4,) * 7 + (spec3, spec3, spec4),
        out_specs=spec4,
        check_vma=False,
    )
```

time: 122 us -> 61.5 us (0.50)
  Pallas kernels: 0 us -> 55.8 us
  local copies, waits for them, and re-layouts: 38.4 us -> 5.25 us
  starting transfers between devices: 33.1 us -> 0 us
  matrix products: 21.1 us -> 0 us
  blocking collectives: 16.5 us -> 0 us
  other arithmetic: 7.85 us -> 0 us
  waiting for transfers between devices: 3.93 us -> 0 us
    pallas_call x0 -> x1, Pallas kernels: none -> 55.8 us  [per_device(): pl.pallas_call(functools.partial(kernel, n_wide, n_narrow, shifts), out_s...]
    ppermute x6 -> x0, starting transfers between devices: 33.1 us -> none  [from_behind(): return lax.ppermute(value, axis, pairs)]
    dot_general x8 -> x0, matrix products: 21.1 us -> none  [the longest x4 16.9 us: add_group(): jnp.einsum('gij,gjk->gik', left_mat[sl], right_mat[sr], preferred_element...]
    all_to_all x1 -> x0, blocking collectives: 16.5 us -> none  [per_device(): lax.all_to_all(outgoing, 'wide', split_axis=0, concat_axis=0, tiled=True)]
    dot_general x4 -> x0, local copies, waits for them, and re-layouts: 15.3 us -> none  [add_group(): jnp.einsum('gij,gjk->gik', left_mat[sl], right_mat[sr], preferred_element...]
    gather x10 -> x0, local copies, waits for them, and re-layouts: 15.1 us -> none  [the longest x4 7.49 us: add_group(): left_mat[sl]]
    lt x4 -> x0, other arithmetic: 4.24 us -> none  [add_group(): live = slots < count]
    ppermute x6 -> x0, waiting for transfers between devices: 3.93 us -> none  [from_behind(): return lax.ppermute(value, axis, pairs)]
  transfers between devices with their start and end apart: 6 -> 0, of which waited for: 2 -> 0; matrix products, arithmetic and copies ran while one was open for 34% -> 0% of each run, Pallas kernels for 0% -> 0%
where the time goes in v1:
time: 61.5 us; the launch traced here: 61.1 us
  Pallas kernels  55.8 us (91%)
  local copies, waits for them, and re-layouts  5.25 us (9%)
    pallas_call x1, Pallas kernels, per_device(): pl.pallas_call(functools.partial(kernel, n_wide, n_narrow, shifts), out_s...  55.8 us
    unnamed x20, local copies, waits for them, and re-layouts  4.43 us

profile of v1, /device:TPU:1, one launch (start us, length us, event | category | flops | bytes accessed | tf_op | source)
XLA Modules:
  0.0 61.1 jit_solution(9440586617912748921)
XLA Ops:
  0.0 0.0 copy-start.6
  0.0 0.0 copy-start.5
  0.0 0.0 copy-start.4
  0.0 0.0 copy-start.7
  0.0 0.0 copy-start.8
  0.0 0.0 copy-start.9
  0.0 0.6 %copy-done.6 = s32[1,1,4,128]{3,2,1,0:T(4,128)S(1)} copy-done((s32[1,1,4,128]{3,2,1,0:T(4,128)S(1)}, s32[1,1,4,128]{3,2,1,0:T(4,128)}, u32[]{:S(2)}) %copy-start.6) | copy-done | bytes 2072
  0.7 0.0 copy-done.5
  0.7 0.0 copy-done.4
  0.7 0.0 copy-done.7
  0.7 0.0 copy-done.8
  0.7 0.0 copy-done.9
  0.7 0.0 copy-start
  0.7 0.9 %copy-done = f32[1,1,16,4096]{3,2,1,0:T(8,128)S(1)} copy-done((f32[1,1,16,4096]{3,2,1,0:T(8,128)S(1)}, f32[1,1,16,4096]{3,2,1,0:T(8,128)}, u32[]{:S(2)}) %copy-start) | copy-done | bytes 262168
  1.7 0.0 copy-start.1
  1.7 0.9 %copy-done.1 = f32[1,1,16,4096]{3,2,1,0:T(8,128)S(1)} copy-done((f32[1,1,16,4096]{3,2,1,0:T(8,128)S(1)}, f32[1,1,16,4096]{3,2,1,0:T(8,128)}, u32[]{:S(2)}) %copy-start.1) | copy-done | bytes 262168
  2.6 0.0 copy-start.2
  2.6 0.9 %copy-done.2 = bf16[1,1,24,4096]{3,2,1,0:T(8,128)(2,1)S(1)} copy-done((bf16[1,1,24,4096]{3,2,1,0:T(8,128)(2,1)S(1)}, bf16[1,1,24,4096]{3,2,1,0:T(8,128)(2,1)}, u32[]{:S(2)}) %copy-start.2) | copy-done | bytes 196632
  3.6 0.0 copy-start.3
  3.6 0.9 %copy-done.3 = bf16[1,1,16,4096]{3,2,1,0:T(8,128)(2,1)S(1)} copy-done((bf16[1,1,16,4096]{3,2,1,0:T(8,128)(2,1)S(1)}, bf16[1,1,16,4096]{3,2,1,0:T(8,128)(2,1)}, u32[]{:S(2)}) %copy-start.3) | copy-done | bytes 131096
  4.5 55.8 %shard_map.100 = bf16[32,32,128]{2,1,0:T(8,128)(2,1)S(1)} custom-call(bf16[24,4096]{1,0:T(8,128)(2,1)S(1)} %bitcast.12, bf16[16,4096]{1,0:T(8,128)(2,1)S(1)} %bitcast.13, f32[16,4096]{1,0:T(8,128)S(1)} %bitcast.10, f32[16,4096]{1,0:T(8,128)S(1)} %bitcast.11, s32[4,128]{1,0:T(4,128)S(1)} %bitcast.14, s32[4,128]{1,0:T(4,128)S(1)} %bitcast.15, ...), custom_call_target="tpu_custom_call" | custom-call | flops 6442450944 | bytes 4194304 | tf_op jit(solution)/shard_map/pallas_call | solution.py:261
  60.3 0.8 %reshape.15 = bf16[1,1,32,4096]{3,2,1,0:T(8,128)(2,1)} reshape(bf16[32,32,128]{2,1,0:T(8,128)(2,1)S(1)} %shard_map.100) | data formatting | bytes 524288 | tf_op jit(solution)/shard_map/reshape | solution.py:296
Async XLA Ops:
  0.0 0.7 %copy-start.6 = (s32[1,1,4,128]{3,2,1,0:T(4,128)S(1)}, s32[1,1,4,128]{3,2,1,0:T(4,128)}, u32[]{:S(2)}) copy-start(s32[1,1,4,128]{3,2,1,0:T(4,128)} %param.16) | copy-start | bytes 6148
  0.0 0.7 %copy-start.5 = (s32[1,1,4,128]{3,2,1,0:T(4,128)S(1)}, s32[1,1,4,128]{3,2,1,0:T(4,128)}, u32[]{:S(2)}) copy-start(s32[1,1,4,128]{3,2,1,0:T(4,128)} %param.15) | copy-start | bytes 6148
  0.0 0.7 %copy-start.4 = (s32[1,1,4,128]{3,2,1,0:T(4,128)S(1)}, s32[1,1,4,128]{3,2,1,0:T(4,128)}, u32[]{:S(2)}) copy-start(s32[1,1,4,128]{3,2,1,0:T(4,128)} %param.14) | copy-start | bytes 6148
  0.0 0.7 %copy-start.7 = (s32[1,1,4]{2,1,0:T(1,128)S(1)}, s32[1,1,4]{2,1,0:T(1,128)}, u32[]{:S(2)}) copy-start(s32[1,1,4]{2,1,0:T(1,128)} %param.17) | copy-start | bytes 52
  0.0 0.7 %copy-start.8 = (s32[1,1,16]{2,1,0:T(1,128)S(1)}, s32[1,1,16]{2,1,0:T(1,128)}, u32[]{:S(2)}) copy-start(s32[1,1,16]{2,1,0:T(1,128)} %param.18) | copy-start | bytes 196
  0.0 0.7 %copy-start.9 = (s32[1,1,32,1]{2,3,1,0:T(1,128)S(1)}, s32[1,1,32,1]{2,3,1,0:T(1,128)}, u32[]{:S(2)}) copy-start(s32[1,1,32,1]{2,3,1,0:T(1,128)} %param.19) | copy-start | bytes 388
  0.7 0.9 %copy-start = (f32[1,1,16,4096]{3,2,1,0:T(8,128)S(1)}, f32[1,1,16,4096]{3,2,1,0:T(8,128)}, u32[]{:S(2)}) copy-start(f32[1,1,16,4096]{3,2,1,0:T(8,128)} %param.12) | copy-start | bytes 786436
  1.7 0.9 %copy-start.1 = (f32[1,1,16,4096]{3,2,1,0:T(8,128)S(1)}, f32[1,1,16,4096]{3,2,1,0:T(8,128)}, u32[]{:S(2)}) copy-start(f32[1,1,16,4096]{3,2,1,0:T(8,128)} %param.13) | copy-start | bytes 786436
  2.6 0.9 %copy-start.2 = (bf16[1,1,24,4096]{3,2,1,0:T(8,128)(2,1)S(1)}, bf16[1,1,24,4096]{3,2,1,0:T(8,128)(2,1)}, u32[]{:S(2)}) copy-start(bf16[1,1,24,4096]{3,2,1,0:T(8,128)(2,1)} %param.10) | copy-start | bytes 589828
  3.6 0.9 %copy-start.3 = (bf16[1,1,16,4096]{3,2,1,0:T(8,128)(2,1)S(1)}, bf16[1,1,16,4096]{3,2,1,0:T(8,128)(2,1)}, u32[]{:S(2)}) copy-start(bf16[1,1,16,4096]{3,2,1,0:T(8,128)(2,1)} %param.11) | copy-start | bytes 393220

commit v2 on v1

v2 whole, which is shorter than its diff:
```python
import functools

import jax
import jax.numpy as jnp
from jax import lax
from jax.experimental import pallas as pl
from jax.experimental.pallas import tpu as pltpu
from jax.sharding import PartitionSpec as P

MESH = pl.DeviceIdType.MESH
EDGE = 64
LANES = 128
VMEM_MIB = 60


def kernel(
    n_wide,
    n_narrow,
    shifts,
    l_ref,
    r_ref,
    e_ref,
    c_ref,
    sl_hbm,
    sr_hbm,
    sc_hbm,
    cnt_hbm,
    keep_hbm,
    send_hbm,
    out_ref,
    sl_ref,
    sr_ref,
    sc_ref,
    cnt_ref,
    keep_ref,
    send_ref,
    lbuf,
    rraw,
    rbuf,
    ebuf,
    cbuf,
    rq,
    rd,
    wsel,
    both,
    wt,
    tot,
    upd,
    rows,
    outgoing,
    lsend,
    lrecv,
    rsend,
    rrecv,
    esem,
    asend,
    arecv,
):
    w = lax.axis_index("wide")
    n = lax.axis_index("narrow")
    nl = l_ref.shape[0]
    nr = r_ref.shape[0]
    nc = e_ref.shape[0]
    tiles = l_ref.shape[1] // LANES
    half = tiles * nc
    bf16, f32 = jnp.bfloat16, jnp.float32

    barrier = pltpu.get_barrier_semaphore()
    for k in range(1, shifts):
        for other in (n + k, n + n_narrow - k):
            pl.semaphore_signal(
                barrier, inc=1, device_id={"narrow": lax.rem(other, n_narrow)}, device_id_type=MESH
            )

    def greet(k, carry):
        pl.semaphore_signal(
            barrier, inc=1, device_id={"wide": lax.rem(w + k, n_wide)}, device_id_type=MESH
        )
        return carry

    lax.fori_loop(1, n_wide, greet, 0)

    get_r = pltpu.make_async_copy(r_ref, rraw, esem.at[0])
    get_r.start()
    own_l = pltpu.make_async_copy(l_ref, lbuf.at[0], lrecv.at[0])
    own_l.start()
    gets = []
    for i, (src, dst) in enumerate(
        (
            (sl_hbm, sl_ref),
            (sr_hbm, sr_ref),
            (sc_hbm, sc_ref),
            (cnt_hbm, cnt_ref),
            (keep_hbm, keep_ref),
            (send_hbm, send_ref),
            (e_ref, ebuf),
            (c_ref, cbuf),
        )
    ):
        copy = pltpu.make_async_copy(src, dst, esem.at[i + 1])
        copy.start()
        gets.append(copy)

    pl.semaphore_wait(barrier, n_wide - 1 + 2 * (shifts - 1))

    l_copies = []
    for k in range(1, shifts):
        copy = pltpu.make_async_remote_copy(
            src_ref=l_ref,
            dst_ref=lbuf.at[k],
            send_sem=lsend.at[k],
            recv_sem=lrecv.at[k],
            device_id={"wide": lax.rem(w + n_wide - k, n_wide)},
            device_id_type=MESH,
        )
        copy.start()
        l_copies.append(copy)

    get_r.wait()
    lane = lax.broadcasted_iota(jnp.int32, (EDGE // 2, LANES), 1)
    low = lane < EDGE
    for t in range(tiles):
        rq[pl.ds(t, nr, stride=tiles), :] = rraw[:, t * LANES : (t + 1) * LANES].astype(f32)
    for p in range(nr // 2):
        even = rq[(2 * p) * tiles : (2 * p + 1) * tiles, :]
        odd = rq[(2 * p + 1) * tiles : (2 * p + 2) * tiles, :]
        rd[pl.ds(p * EDGE, EDGE // 2, stride=2), :] = jnp.where(low, even, pltpu.roll(odd, EDGE, 1))
        rd[pl.ds(p * EDGE + 1, EDGE // 2, stride=2), :] = jnp.where(
            low, pltpu.roll(even, EDGE, 1), odd
        )
    rbuf[0] = rd[...].astype(bf16)

    r_copies = []
    for k in range(1, shifts):
        copy = pltpu.make_async_remote_copy(
            src_ref=rbuf.at[0],
            dst_ref=rbuf.at[k],
            send_sem=rsend.at[k],
            recv_sem=rrecv.at[k],
            device_id={"narrow": lax.rem(n + n_narrow - k, n_narrow)},
            device_id_type=MESH,
        )
        copy.start()
        r_copies.append(copy)

    for copy in gets:
        copy.wait()
    slots = sl_ref.shape[1]
    slot = lax.broadcasted_iota(jnp.int32, (1, slots), 1)
    for s in range(shifts):
        live = slot < cnt_ref[:, s : s + 1]
        cell = jnp.where(live, sr_ref[s : s + 1, :] * nc + sc_ref[s : s + 1, :], -1)
        cells = lax.broadcasted_iota(jnp.int32, (nr * nc, slots), 0) == cell
        lefts = lax.broadcasted_iota(jnp.int32, (nl, slots), 0) == sl_ref[s : s + 1, :]
        wsel[s] = lax.dot_general(
            cells.astype(f32).astype(bf16),
            lefts.astype(f32).astype(bf16),
            (((1,), (1,)), ((), ())),
            preferred_element_type=f32,
        ).astype(bf16)

    tot[...] = jnp.zeros_like(tot)
    low_w = lax.broadcasted_iota(jnp.int32, (EDGE, LANES), 1) < EDGE

    def one_shift(s, carry):
        @pl.when(s > 0)
        def _():
            pltpu.make_async_copy(rbuf.at[s], rbuf.at[s], rrecv.at[s]).wait()

        for p in range(nr // 2):
            pair = rbuf[s, p * EDGE : (p + 1) * EDGE, :].astype(f32)
            turned = pltpu.roll(pair, EDGE, 1)
            base = p * 4 * EDGE
            wt[base : base + EDGE, :] = jnp.where(low_w, pair, 0.0).astype(bf16)
            wt[base + EDGE : base + 2 * EDGE, :] = jnp.where(low_w, 0.0, turned).astype(bf16)
            wt[base + 2 * EDGE : base + 3 * EDGE, :] = jnp.where(low_w, turned, 0.0).astype(bf16)
            wt[base + 3 * EDGE : base + 4 * EDGE, :] = jnp.where(low_w, 0.0, pair).astype(bf16)
        pltpu.make_async_copy(lbuf.at[s], lbuf.at[s], lrecv.at[s]).wait()
        sel = wsel[s]
        for q in range(tiles // 2):
            a = jnp.dot(
                sel, lbuf[s, :, q * 2 * LANES : (q + 1) * 2 * LANES], preferred_element_type=f32
            )
            hi = a.astype(bf16)
            lo = (a - hi.astype(f32)).astype(bf16)
            for h in range(2):
                at = (2 * q + h) * nc
                for r in range(nr):
                    src = (slice(r * nc, (r + 1) * nc), slice(h * LANES, (h + 1) * LANES))
                    both[at : at + nc, r * LANES : (r + 1) * LANES] = hi[src]
                    both[half + at : half + at + nc, r * LANES : (r + 1) * LANES] = lo[src]
        v = jnp.dot(both[...], wt[...], preferred_element_type=f32)
        tot[...] += v[:half] + v[half:]
        return carry

    lax.fori_loop(0, shifts, one_shift, 0)

    eye = lax.broadcasted_iota(jnp.int32, (nc, nc), 0) == lax.broadcasted_iota(jnp.int32, (nc, nc), 1)
    keep = jnp.sum(jnp.where(eye, keep_ref[...].astype(f32), 0.0), axis=1, keepdims=True)
    for t in range(tiles):
        cols = slice(t * LANES, (t + 1) * LANES)
        total = ebuf[:, cols] + tot[t * nc : (t + 1) * nc, :]
        upd[:, cols] = ((1.5 * cbuf[:, cols] - 0.5 * total) * keep).astype(bf16)
    eye_w = lax.broadcasted_iota(jnp.int32, (n_wide, n_wide), 0) == lax.broadcasted_iota(
        jnp.int32, (n_wide, n_wide), 1
    )
    sends = jnp.sum(jnp.where(eye_w, send_ref[...].astype(f32), 0.0), axis=1, keepdims=True)
    pick = (
        (lax.broadcasted_iota(jnp.int32, (n_wide, nc), 1) == sends.astype(jnp.int32))
        .astype(f32)
        .astype(bf16)
    )
    for t in range(0, tiles, 4):
        picked = jnp.dot(pick, upd[:, t * LANES : (t + 4) * LANES], preferred_element_type=f32)
        for h in range(4):
            rows[pl.ds(t + h, n_wide, stride=tiles), :] = picked[:, h * LANES : (h + 1) * LANES]

    def send_block(k, carry):
        d = lax.rem(w + k, n_wide)
        outgoing[d] = rows[pl.ds(pl.multiple_of(d * tiles, tiles), tiles), :].astype(bf16)
        pltpu.make_async_remote_copy(
            src_ref=outgoing.at[d],
            dst_ref=out_ref.at[w],
            send_sem=asend.at[0],
            recv_sem=arecv.at[0],
            device_id={"wide": d},
            device_id_type=MESH,
        ).start()
        return carry

    lax.fori_loop(1, n_wide, send_block, 0)
    outgoing[w] = rows[pl.ds(pl.multiple_of(w * tiles, tiles), tiles), :].astype(bf16)
    pltpu.make_async_copy(outgoing.at[w], out_ref.at[w], arecv.at[0]).start()

    for copy in l_copies:
        copy.wait_send()
    for copy in r_copies:
        copy.wait_send()
    others = outgoing.at[pl.ds(0, n_wide - 1)]
    pltpu.make_async_copy(others, others, asend.at[0]).wait()
    pltpu.make_async_copy(outgoing, outgoing, arecv.at[0]).wait()


def per_device(n_wide, n_narrow, left, right, earlier, current, sl, sr, sc, count, keep, send):
    left, right, earlier, current = left[0, 0], right[0, 0], earlier[0, 0], current[0, 0]
    sl, sr, sc = sl[0, 0], sr[0, 0], sc[0, 0]
    shifts, slots = sl.shape
    nl, flat = left.shape
    nr = right.shape[0]
    nc = earlier.shape[0]
    tiles = flat // LANES
    count = count.reshape(1, shifts)
    keep = keep.reshape(1, nc)
    send = send.reshape(1, n_wide)
    bf16, f32, i32 = jnp.bfloat16, jnp.float32, jnp.int32
    hbm = pl.BlockSpec(memory_space=pl.ANY)
    dma = pltpu.SemaphoreType.DMA
    out = pl.pallas_call(
        functools.partial(kernel, n_wide, n_narrow, shifts),
        out_shape=jax.ShapeDtypeStruct((n_wide, tiles, LANES), bf16),
        in_specs=[hbm] * 10,
        out_specs=hbm,
        scratch_shapes=[
            pltpu.VMEM((shifts, slots), i32),
            pltpu.VMEM((shifts, slots), i32),
            pltpu.VMEM((shifts, slots), i32),
            pltpu.VMEM((1, shifts), i32),
            pltpu.VMEM((1, nc), i32),
            pltpu.VMEM((1, n_wide), i32),
            pltpu.VMEM((shifts, nl, flat), bf16),
            pltpu.VMEM((nr, flat), bf16),
            pltpu.VMEM((shifts, nr // 2 * EDGE, LANES), bf16),
            pltpu.VMEM((nc, flat), f32),
            pltpu.VMEM((nc, flat), f32),
            pltpu.VMEM((nr * tiles, LANES), f32),
            pltpu.VMEM((nr // 2 * EDGE, LANES), f32),
            pltpu.VMEM((shifts, nr * nc, nl), bf16),
            pltpu.VMEM((2 * tiles * nc, nr * LANES), bf16),
            pltpu.VMEM((nr * LANES, LANES), bf16),
            pltpu.VMEM((tiles * nc, LANES), f32),
            pltpu.VMEM((nc, flat), bf16),
            pltpu.VMEM((n_wide * tiles, LANES), f32),
            pltpu.VMEM((n_wide, tiles, LANES), bf16),
            dma((shifts,)),
            dma((shifts,)),
            dma((shifts,)),
            dma((shifts,)),
            dma((9,)),
            dma((1,)),
            dma((1,)),
        ],
        compiler_params=pltpu.CompilerParams(
            collective_id=0, has_side_effects=True, vmem_limit_bytes=VMEM_MIB * 1024 * 1024
        ),
        cost_estimate=pl.CostEstimate(
            flops=2 * shifts * flat * 256 * 256 * 3, bytes_accessed=4 << 20, transcendentals=0
        ),
    )(left, right, earlier, current, sl, sr, sc, count, keep, send)
    return out.reshape(1, 1, n_wide, flat)


def solution(mesh):
    spec4 = P("wide", "narrow", None, None)
    spec3 = P("wide", "narrow", None)
    return jax.shard_map(
        functools.partial(per_device, mesh.shape["wide"], mesh.shape["narrow"]),
        mesh=mesh,
        in_specs=(spec4,) * 7 + (spec3, spec3, spec4),
        out_specs=spec4,
        check_vma=False,
    )
```

time: 61.5 us -> 47.8 us (0.78)
  Pallas kernels: 55.8 us -> 45.8 us
  local copies, waits for them, and re-layouts: 5.25 us -> 1.77 us
    pallas_call x1, Pallas kernels: 55.8 us -> 45.8 us  [per_device(): pl.pallas_call(functools.partial(kernel, n_wide, n_narrow, shifts), out_s...]
    unnamed x20 -> x0, local copies, waits for them, and re-layouts: 4.43 us -> none
    reshape x1, local copies, waits for them, and re-layouts: 0.82 us -> 1.77 us  [per_device(): return out.reshape(1, 1, n_wide, flat)]
where the time goes in v2:
time: 47.8 us; the launch traced here: 47.6 us
  Pallas kernels  45.8 us (96%)
  local copies, waits for them, and re-layouts  1.77 us (4%)
    pallas_call x1, Pallas kernels, per_device(): pl.pallas_call(functools.partial(kernel, n_wide, n_narrow, shifts), out_s...  45.8 us
    reshape x1, local copies, waits for them, and re-layouts, per_device(): return out.reshape(1, 1, n_wide, flat)  1.77 us

profile of v2, /device:TPU:1, one launch (start us, length us, event | category | flops | bytes accessed | tf_op | source)
XLA Modules:
  0.0 47.6 jit_solution(11132438854735593082)
XLA Ops:
  0.0 45.8 %shard_map.100 = bf16[32,32,128]{2,1,0:T(8,128)(2,1)} custom-call(bf16[24,4096]{1,0:T(8,128)(2,1)} %bitcast.12, bf16[16,4096]{1,0:T(8,128)(2,1)} %bitcast.13, f32[16,4096]{1,0:T(8,128)} %bitcast.10, f32[16,4096]{1,0:T(8,128)} %bitcast.11, s32[4,128]{1,0:T(4,128)} %bitcast.14, s32[4,128]{1,0:T(4,128)} %bitcast.15, s32[4,128]{1,0:T(4,128)} %bitcast.16, ...), custom_call_target="tpu_custom_call" | custom-call | flops 6442450944 | bytes 4194304 | tf_op jit(solution)/shard_map/pallas_call | solution.py:258
  45.8 1.8 %reshape.15 = bf16[1,1,32,4096]{3,2,1,0:T(8,128)(2,1)} reshape(bf16[32,32,128]{2,1,0:T(8,128)(2,1)} %shard_map.100) | data formatting | bytes 524288 | tf_op jit(solution)/shard_map/reshape | solution.py:299

commit v3 on v2

--- a/solution.py
+++ b/solution.py
@@ -10,7 +10,8 @@
 MESH = pl.DeviceIdType.MESH
 EDGE = 64
 LANES = 128
-VMEM_MIB = 60
+VMEM_MIB = 56
+RELAY = 1
 
 
 def kernel(
@@ -66,7 +67,7 @@
     bf16, f32 = jnp.bfloat16, jnp.float32
 
     barrier = pltpu.get_barrier_semaphore()
-    for k in range(1, shifts):
+    for k in range(1, shifts - 1):
         for other in (n + k, n + n_narrow - k):
             pl.semaphore_signal(
                 barrier, inc=1, device_id={"narrow": lax.rem(other, n_narrow)}, device_id_type=MESH
@@ -101,20 +102,25 @@
         copy.start()
         gets.append(copy)
 
-    pl.semaphore_wait(barrier, n_wide - 1 + 2 * (shifts - 1))
-
-    l_copies = []
-    for k in range(1, shifts):
-        copy = pltpu.make_async_remote_copy(
-            src_ref=l_ref,
-            dst_ref=lbuf.at[k],
-            send_sem=lsend.at[k],
-            recv_sem=lrecv.at[k],
-            device_id={"wide": lax.rem(w + n_wide - k, n_wide)},
+    pl.semaphore_wait(barrier, n_wide - 1 + 2 * (shifts - 2))
+
+    odd = lax.rem(w, 2)
+
+    def send_left(src, slot, to, sem):
+        return pltpu.make_async_remote_copy(
+            src_ref=src,
+            dst_ref=lbuf.at[slot],
+            send_sem=lsend.at[sem],
+            recv_sem=lrecv.at[slot],
+            device_id={"wide": lax.rem(to + n_wide, n_wide)},
             device_id_type=MESH,
         )
-        copy.start()
-        l_copies.append(copy)
+
+    left_two = send_left(l_ref, 2, w - 2, 0)
+    left_two.start()
+    left_near = send_left(l_ref, 3 - 2 * odd, w - 3 + 2 * odd, 1)
+    left_near.start()
+    left_on = send_left(lbuf.at[2], 1 + 2 * odd, w + 1 - 2 * odd, 2)
 
     get_r.wait()
     lane = lax.broadcasted_iota(jnp.int32, (EDGE // 2, LANES), 1)
@@ -130,18 +136,21 @@
         )
     rbuf[0] = rd[...].astype(bf16)
 
-    r_copies = []
-    for k in range(1, shifts):
-        copy = pltpu.make_async_remote_copy(
-            src_ref=rbuf.at[0],
-            dst_ref=rbuf.at[k],
-            send_sem=rsend.at[k],
-            recv_sem=rrecv.at[k],
-            device_id={"narrow": lax.rem(n + n_narrow - k, n_narrow)},
+    def send_right(src, slot, back, sem):
+        return pltpu.make_async_remote_copy(
+            src_ref=rbuf.at[src],
+            dst_ref=rbuf.at[slot],
+            send_sem=rsend.at[sem],
+            recv_sem=rrecv.at[slot],
+            device_id={"narrow": lax.rem(n + n_narrow - back, n_narrow)},
             device_id_type=MESH,
         )
-        copy.start()
-        r_copies.append(copy)
+
+    right_one = send_right(0, 1, 1, 0)
+    right_one.start()
+    right_two = send_right(0, 2, 2, 1)
+    right_two.start()
+    right_on = send_right(1, 3, 2, 2)
 
     for copy in gets:
         copy.wait()
@@ -162,10 +171,20 @@
     tot[...] = jnp.zeros_like(tot)
     low_w = lax.broadcasted_iota(jnp.int32, (EDGE, LANES), 1) < EDGE
 
-    def one_shift(s, carry):
-        @pl.when(s > 0)
+    def one_shift(i, carry):
+        s = i // 2 + 2 * lax.rem(i, 2)
+
+        @pl.when(i == 1)
         def _():
-            pltpu.make_async_copy(rbuf.at[s], rbuf.at[s], rrecv.at[s]).wait()
+            pltpu.make_async_copy(rbuf.at[1], rbuf.at[1], rrecv.at[1]).wait()
+            right_on.start()
+            pltpu.make_async_copy(lbuf.at[2], lbuf.at[2], lrecv.at[2]).wait()
+            left_on.start()
+            pltpu.make_async_copy(rbuf.at[2], rbuf.at[2], rrecv.at[2]).wait()
+
+        @pl.when(i == 3)
+        def _():
+            pltpu.make_async_copy(rbuf.at[3], rbuf.at[3], rrecv.at[3]).wait()
 
         for p in range(nr // 2):
             pair = rbuf[s, p * EDGE : (p + 1) * EDGE, :].astype(f32)
@@ -175,7 +194,11 @@
             wt[base + EDGE : base + 2 * EDGE, :] = jnp.where(low_w, 0.0, turned).astype(bf16)
             wt[base + 2 * EDGE : base + 3 * EDGE, :] = jnp.where(low_w, turned, 0.0).astype(bf16)
             wt[base + 3 * EDGE : base + 4 * EDGE, :] = jnp.where(low_w, 0.0, pair).astype(bf16)
-        pltpu.make_async_copy(lbuf.at[s], lbuf.at[s], lrecv.at[s]).wait()
+
+        @pl.when(i != 1)
+        def _():
+            pltpu.make_async_copy(lbuf.at[s], lbuf.at[s], lrecv.at[s]).wait()
+
         sel = wsel[s]
         for q in range(tiles // 2):
             a = jnp.dot(
@@ -232,9 +255,7 @@
     outgoing[w] = rows[pl.ds(pl.multiple_of(w * tiles, tiles), tiles), :].astype(bf16)
     pltpu.make_async_copy(outgoing.at[w], out_ref.at[w], arecv.at[0]).start()
 
-    for copy in l_copies:
-        copy.wait_send()
-    for copy in r_copies:
+    for copy in (left_two, left_near, left_on, right_one, right_two, right_on):
         copy.wait_send()
     others = outgoing.at[pl.ds(0, n_wide - 1)]
     pltpu.make_async_copy(others, others, asend.at[0]).wait()
@@ -254,12 +275,17 @@
     send = send.reshape(1, n_wide)
     bf16, f32, i32 = jnp.bfloat16, jnp.float32, jnp.int32
     hbm = pl.BlockSpec(memory_space=pl.ANY)
+    vmem = pl.BlockSpec(memory_space=pltpu.VMEM)
     dma = pltpu.SemaphoreType.DMA
+    operands = [
+        pltpu.with_memory_space_constraint(x, pltpu.HBM)
+        for x in (left, right, earlier, current, sl, sr, sc, count, keep, send)
+    ]
     out = pl.pallas_call(
         functools.partial(kernel, n_wide, n_narrow, shifts),
-        out_shape=jax.ShapeDtypeStruct((n_wide, tiles, LANES), bf16),
+        out_shape=pltpu.VMEM((n_wide, tiles, LANES), bf16),
         in_specs=[hbm] * 10,
-        out_specs=hbm,
+        out_specs=vmem,
         scratch_shapes=[
             pltpu.VMEM((shifts, slots), i32),
             pltpu.VMEM((shifts, slots), i32),
@@ -295,7 +321,7 @@
         cost_estimate=pl.CostEstimate(
             flops=2 * shifts * flat * 256 * 256 * 3, bytes_accessed=4 << 20, transcendentals=0
         ),
-    )(left, right, earlier, current, sl, sr, sc, count, keep, send)
+    )(*operands)
     return out.reshape(1, 1, n_wide, flat)
 
 

time: 47.8 us -> 40.9 us (0.86)
  the two profiles are of different devices: /device:TPU:1 before, /device:TPU:27 now
where the time goes in v3:
time: 40.9 us; the launch traced here: 40.8 us
  Pallas kernels  39.9 us (98%)
  local copies, waits for them, and re-layouts  0.82 us (2%)
    pallas_call x1, Pallas kernels, per_device(): pl.pallas_call(functools.partial(kernel, n_wide, n_narrow, shifts), out_s...  39.9 us

profile of v3, /device:TPU:27, one launch (start us, length us, event | category | flops | bytes accessed | tf_op | source)
XLA Modules:
  0.0 40.8 jit_solution(12854301444215967713)
XLA Ops:
  0.0 39.9 %shard_map.100 = bf16[32,32,128]{2,1,0:T(8,128)(2,1)S(1)} custom-call(bf16[24,4096]{1,0:T(8,128)(2,1)} %bitcast.12, bf16[16,4096]{1,0:T(8,128)(2,1)} %bitcast.13, f32[16,4096]{1,0:T(8,128)} %bitcast.10, f32[16,4096]{1,0:T(8,128)} %bitcast.11, s32[4,128]{1,0:T(4,128)} %bitcast.14, s32[4,128]{1,0:T(4,128)} %bitcast.15, s32[4,128]{1,0:T(4,128)} %bitcast.16, ...), custom_call_target="tpu_custom_call" | custom-call | flops 6442450944 | bytes 4194304 | tf_op jit(solution)/shard_map/pallas_call | solution.py:284
  40.0 0.8 %reshape.15 = bf16[1,1,32,4096]{3,2,1,0:T(8,128)(2,1)} reshape(bf16[32,32,128]{2,1,0:T(8,128)(2,1)S(1)} %shard_map.100) | data formatting | bytes 524288 | tf_op jit(solution)/shard_map/reshape | solution.py:325

commit v4 on v3

--- a/solution.py
+++ b/solution.py
@@ -11,7 +11,7 @@
 EDGE = 64
 LANES = 128
 VMEM_MIB = 56
-RELAY = 1
+PARTS = 4
 
 
 def kernel(
@@ -66,6 +66,8 @@
     half = tiles * nc
     bf16, f32 = jnp.bfloat16, jnp.float32
 
+    get_r = pltpu.make_async_copy(r_ref, rraw, esem.at[0])
+    get_r.start()
     barrier = pltpu.get_barrier_semaphore()
     for k in range(1, shifts - 1):
         for other in (n + k, n + n_narrow - k):
@@ -81,9 +83,7 @@
 
     lax.fori_loop(1, n_wide, greet, 0)
 
-    get_r = pltpu.make_async_copy(r_ref, rraw, esem.at[0])
-    get_r.start()
-    own_l = pltpu.make_async_copy(l_ref, lbuf.at[0], lrecv.at[0])
+    own_l = pltpu.make_async_copy(l_ref, lbuf.at[0], esem.at[9])
     own_l.start()
     gets = []
     for i, (src, dst) in enumerate(
@@ -102,26 +102,6 @@
         copy.start()
         gets.append(copy)
 
-    pl.semaphore_wait(barrier, n_wide - 1 + 2 * (shifts - 2))
-
-    odd = lax.rem(w, 2)
-
-    def send_left(src, slot, to, sem):
-        return pltpu.make_async_remote_copy(
-            src_ref=src,
-            dst_ref=lbuf.at[slot],
-            send_sem=lsend.at[sem],
-            recv_sem=lrecv.at[slot],
-            device_id={"wide": lax.rem(to + n_wide, n_wide)},
-            device_id_type=MESH,
-        )
-
-    left_two = send_left(l_ref, 2, w - 2, 0)
-    left_two.start()
-    left_near = send_left(l_ref, 3 - 2 * odd, w - 3 + 2 * odd, 1)
-    left_near.start()
-    left_on = send_left(lbuf.at[2], 1 + 2 * odd, w + 1 - 2 * odd, 2)
-
     get_r.wait()
     lane = lax.broadcasted_iota(jnp.int32, (EDGE // 2, LANES), 1)
     low = lane < EDGE
@@ -136,21 +116,49 @@
         )
     rbuf[0] = rd[...].astype(bf16)
 
-    def send_right(src, slot, back, sem):
+    odd = lax.rem(w, 2)
+
+    def send_left(src, slot, to, sem):
         return pltpu.make_async_remote_copy(
-            src_ref=rbuf.at[src],
-            dst_ref=rbuf.at[slot],
-            send_sem=rsend.at[sem],
-            recv_sem=rrecv.at[slot],
+            src_ref=src,
+            dst_ref=lbuf.at[slot],
+            send_sem=lsend.at[sem],
+            recv_sem=lrecv.at[slot],
+            device_id={"wide": lax.rem(to + n_wide, n_wide)},
+            device_id_type=MESH,
+        )
+
+    def got_left(slot):
+        return pltpu.make_async_copy(lbuf.at[slot], lbuf.at[slot], lrecv.at[slot])
+
+    left_one = send_left(l_ref, 1, w - 1, 0)
+    left_three = send_left(l_ref, 3, w - 3, 1)
+    left_on = send_left(lbuf.at[3 - 2 * odd], 2, w + 1 - 2 * odd, 2)
+
+    part = rbuf.shape[1] // PARTS
+
+    def send_right(src, slot, back, sem, c):
+        at = slice(c * part, (c + 1) * part)
+        return pltpu.make_async_remote_copy(
+            src_ref=rbuf.at[src, at],
+            dst_ref=rbuf.at[slot, at],
+            send_sem=rsend.at[sem, c],
+            recv_sem=rrecv.at[slot, c],
             device_id={"narrow": lax.rem(n + n_narrow - back, n_narrow)},
             device_id_type=MESH,
         )
 
-    right_one = send_right(0, 1, 1, 0)
-    right_one.start()
-    right_two = send_right(0, 2, 2, 1)
-    right_two.start()
-    right_on = send_right(1, 3, 2, 2)
+    def got_right(slot, c):
+        ref = rbuf.at[slot, c * part : (c + 1) * part]
+        return pltpu.make_async_copy(ref, ref, rrecv.at[slot, c])
+
+    right_one = [send_right(0, 1, 1, 0, c) for c in range(PARTS)]
+    right_two = [send_right(0, 2, 2, 1, c) for c in range(PARTS)]
+    right_on = [send_right(1, 3, 2, 2, c) for c in range(PARTS)]
+
+    pl.semaphore_wait(barrier, n_wide - 1 + 2 * (shifts - 2))
+    for copy in right_one + [left_one]:
+        copy.start()
 
     for copy in gets:
         copy.wait()
@@ -172,32 +180,35 @@
     low_w = lax.broadcasted_iota(jnp.int32, (EDGE, LANES), 1) < EDGE
 
     def one_shift(i, carry):
-        s = i // 2 + 2 * lax.rem(i, 2)
+        s = jnp.where(i < 2, i, 2 + lax.rem(i + odd, 2))
 
         @pl.when(i == 1)
         def _():
-            pltpu.make_async_copy(rbuf.at[1], rbuf.at[1], rrecv.at[1]).wait()
-            right_on.start()
-            pltpu.make_async_copy(lbuf.at[2], lbuf.at[2], lrecv.at[2]).wait()
-            left_on.start()
-            pltpu.make_async_copy(rbuf.at[2], rbuf.at[2], rrecv.at[2]).wait()
-
-        @pl.when(i == 3)
+            for copy in right_one:
+                copy.wait_send()
+            for copy in [left_three] + right_two:
+                copy.start()
+            for c in range(PARTS):
+                got_right(1, c).wait()
+                right_on[c].start()
+            got_left(1).wait()
+
+            @pl.when(odd == 1)
+            def _():
+                left_on.start()
+
+        @pl.when(i == 2)
         def _():
-            pltpu.make_async_copy(rbuf.at[3], rbuf.at[3], rrecv.at[3]).wait()
-
-        for p in range(nr // 2):
-            pair = rbuf[s, p * EDGE : (p + 1) * EDGE, :].astype(f32)
-            turned = pltpu.roll(pair, EDGE, 1)
-            base = p * 4 * EDGE
-            wt[base : base + EDGE, :] = jnp.where(low_w, pair, 0.0).astype(bf16)
-            wt[base + EDGE : base + 2 * EDGE, :] = jnp.where(low_w, 0.0, turned).astype(bf16)
-            wt[base + 2 * EDGE : base + 3 * EDGE, :] = jnp.where(low_w, turned, 0.0).astype(bf16)
-            wt[base + 3 * EDGE : base + 4 * EDGE, :] = jnp.where(low_w, 0.0, pair).astype(bf16)
-
-        @pl.when(i != 1)
+            got_left(3).wait()
+
+            @pl.when(odd == 0)
+            def _():
+                left_on.start()
+                got_left(2).wait()
+
+        @pl.when((i == 3) & (odd == 1))
         def _():
-            pltpu.make_async_copy(lbuf.at[s], lbuf.at[s], lrecv.at[s]).wait()
+            got_left(2).wait()
 
         sel = wsel[s]
         for q in range(tiles // 2):
@@ -212,10 +223,25 @@
                     src = (slice(r * nc, (r + 1) * nc), slice(h * LANES, (h + 1) * LANES))
                     both[at : at + nc, r * LANES : (r + 1) * LANES] = hi[src]
                     both[half + at : half + at + nc, r * LANES : (r + 1) * LANES] = lo[src]
+
+        @pl.when(i > 1)
+        def _():
+            for c in range(PARTS):
+                got_right(s, c).wait()
+
+        for p in range(nr // 2):
+            pair = rbuf[s, p * EDGE : (p + 1) * EDGE, :].astype(f32)
+            turned = pltpu.roll(pair, EDGE, 1)
+            base = p * 4 * EDGE
+            wt[base : base + EDGE, :] = jnp.where(low_w, pair, 0.0).astype(bf16)
+            wt[base + EDGE : base + 2 * EDGE, :] = jnp.where(low_w, 0.0, turned).astype(bf16)
+            wt[base + 2 * EDGE : base + 3 * EDGE, :] = jnp.where(low_w, turned, 0.0).astype(bf16)
+            wt[base + 3 * EDGE : base + 4 * EDGE, :] = jnp.where(low_w, 0.0, pair).astype(bf16)
         v = jnp.dot(both[...], wt[...], preferred_element_type=f32)
         tot[...] += v[:half] + v[half:]
         return carry
 
+    own_l.wait()
     lax.fori_loop(0, shifts, one_shift, 0)
 
     eye = lax.broadcasted_iota(jnp.int32, (nc, nc), 0) == lax.broadcasted_iota(jnp.int32, (nc, nc), 1)
@@ -255,7 +281,7 @@
     outgoing[w] = rows[pl.ds(pl.multiple_of(w * tiles, tiles), tiles), :].astype(bf16)
     pltpu.make_async_copy(outgoing.at[w], out_ref.at[w], arecv.at[0]).start()
 
-    for copy in (left_two, left_near, left_on, right_one, right_two, right_on):
+    for copy in [left_one, left_three, left_on] + right_two + right_on:
         copy.wait_send()
     others = outgoing.at[pl.ds(0, n_wide - 1)]
     pltpu.make_async_copy(others, others, asend.at[0]).wait()
@@ -307,11 +333,11 @@
             pltpu.VMEM((nc, flat), bf16),
             pltpu.VMEM((n_wide * tiles, LANES), f32),
             pltpu.VMEM((n_wide, tiles, LANES), bf16),
+            dma((3,)),
             dma((shifts,)),
-            dma((shifts,)),
-            dma((shifts,)),
-            dma((shifts,)),
-            dma((9,)),
+            dma((3, PARTS)),
+            dma((shifts, PARTS)),
+            dma((10,)),
             dma((1,)),
             dma((1,)),
         ],

time: 40.9 us -> 39.1 us (0.956)
  the two profiles are of different devices: /device:TPU:27 before, /device:TPU:1 now
where the time goes in v4:
time: 39.1 us; the launch traced here: 39 us
  Pallas kernels  38.2 us (98%)
  local copies, waits for them, and re-layouts  0.82 us (2%)
    pallas_call x1, Pallas kernels, per_device(): pl.pallas_call(functools.partial(kernel, n_wide, n_narrow, shifts), out_s...  38.2 us
    reshape x1, local copies, waits for them, and re-layouts, per_device(): return out.reshape(1, 1, n_wide, flat)  0.82 us

profile of v4, /device:TPU:1, one launch (start us, length us, event | category | flops | bytes accessed | tf_op | source)
XLA Modules:
  0.0 39.0 jit_solution(8979855264013427564)
XLA Ops:
  0.0 38.2 %shard_map.100 = bf16[32,32,128]{2,1,0:T(8,128)(2,1)S(1)} custom-call(bf16[24,4096]{1,0:T(8,128)(2,1)} %bitcast.12, bf16[16,4096]{1,0:T(8,128)(2,1)} %bitcast.13, f32[16,4096]{1,0:T(8,128)} %bitcast.10, f32[16,4096]{1,0:T(8,128)} %bitcast.11, s32[4,128]{1,0:T(4,128)} %bitcast.14, s32[4,128]{1,0:T(4,128)} %bitcast.15, s32[4,128]{1,0:T(4,128)} %bitcast.16, ...), custom_call_target="tpu_custom_call" | custom-call | flops 6442450944 | bytes 4194304 | tf_op jit(solution)/shard_map/pallas_call | solution.py:310
  38.2 0.8 %reshape.15 = bf16[1,1,32,4096]{3,2,1,0:T(8,128)(2,1)} reshape(bf16[32,32,128]{2,1,0:T(8,128)(2,1)S(1)} %shard_map.100) | data formatting | bytes 524288 | tf_op jit(solution)/shard_map/reshape | solution.py:351

commit v5 on v4

--- a/solution.py
+++ b/solution.py
@@ -12,6 +12,7 @@
 LANES = 128
 VMEM_MIB = 56
 PARTS = 4
+SPLIT = 2
 
 
 def kernel(
@@ -48,6 +49,8 @@
     tot,
     upd,
     rows,
+    keeps,
+    picks,
     outgoing,
     lsend,
     lrecv,
@@ -56,6 +59,7 @@
     esem,
     asend,
     arecv,
+    word,
 ):
     w = lax.axis_index("wide")
     n = lax.axis_index("narrow")
@@ -63,7 +67,6 @@
     nr = r_ref.shape[0]
     nc = e_ref.shape[0]
     tiles = l_ref.shape[1] // LANES
-    half = tiles * nc
     bf16, f32 = jnp.bfloat16, jnp.float32
 
     get_r = pltpu.make_async_copy(r_ref, rraw, esem.at[0])
@@ -75,13 +78,26 @@
                 barrier, inc=1, device_id={"narrow": lax.rem(other, n_narrow)}, device_id_type=MESH
             )
 
-    def greet(k, carry):
-        pl.semaphore_signal(
-            barrier, inc=1, device_id={"wide": lax.rem(w + k, n_wide)}, device_id_type=MESH
-        )
-        return carry
-
-    lax.fori_loop(1, n_wide, greet, 0)
+    for k in range(1, shifts):
+        for other in (w + k, w + n_wide - k):
+            pl.semaphore_signal(
+                barrier, inc=1, device_id={"wide": lax.rem(other, n_wide)}, device_id_type=MESH
+            )
+
+    words = []
+    reach = shifts - 1
+    while 2 * reach + 1 < n_wide:
+        words.append(reach)
+        reach *= 2
+
+    def say(i):
+        for other in (w + words[i], w + n_wide - words[i]):
+            pl.semaphore_signal(
+                word.at[i], inc=1, device_id={"wide": lax.rem(other, n_wide)}, device_id_type=MESH
+            )
+
+    def hear(i):
+        pl.semaphore_wait(word.at[i], 2)
 
     own_l = pltpu.make_async_copy(l_ref, lbuf.at[0], esem.at[9])
     own_l.start()
@@ -102,20 +118,6 @@
         copy.start()
         gets.append(copy)
 
-    get_r.wait()
-    lane = lax.broadcasted_iota(jnp.int32, (EDGE // 2, LANES), 1)
-    low = lane < EDGE
-    for t in range(tiles):
-        rq[pl.ds(t, nr, stride=tiles), :] = rraw[:, t * LANES : (t + 1) * LANES].astype(f32)
-    for p in range(nr // 2):
-        even = rq[(2 * p) * tiles : (2 * p + 1) * tiles, :]
-        odd = rq[(2 * p + 1) * tiles : (2 * p + 2) * tiles, :]
-        rd[pl.ds(p * EDGE, EDGE // 2, stride=2), :] = jnp.where(low, even, pltpu.roll(odd, EDGE, 1))
-        rd[pl.ds(p * EDGE + 1, EDGE // 2, stride=2), :] = jnp.where(
-            low, pltpu.roll(even, EDGE, 1), odd
-        )
-    rbuf[0] = rd[...].astype(bf16)
-
     odd = lax.rem(w, 2)
 
     def send_left(src, slot, to, sem):
@@ -134,6 +136,21 @@
     left_one = send_left(l_ref, 1, w - 1, 0)
     left_three = send_left(l_ref, 3, w - 3, 1)
     left_on = send_left(lbuf.at[3 - 2 * odd], 2, w + 1 - 2 * odd, 2)
+
+
+    get_r.wait()
+    lane = lax.broadcasted_iota(jnp.int32, (EDGE // 2, LANES), 1)
+    low = lane < EDGE
+    for t in range(tiles):
+        rq[pl.ds(t, nr, stride=tiles), :] = rraw[:, t * LANES : (t + 1) * LANES].astype(f32)
+    for p in range(nr // 2):
+        first = rq[(2 * p) * tiles : (2 * p + 1) * tiles, :]
+        second = rq[(2 * p + 1) * tiles : (2 * p + 2) * tiles, :]
+        rd[pl.ds(p * EDGE, EDGE // 2, stride=2), :] = jnp.where(low, first, pltpu.roll(second, EDGE, 1))
+        rd[pl.ds(p * EDGE + 1, EDGE // 2, stride=2), :] = jnp.where(
+            low, pltpu.roll(first, EDGE, 1), second
+        )
+    rbuf[0] = rd[...].astype(bf16)
 
     part = rbuf.shape[1] // PARTS
 
@@ -156,9 +173,12 @@
     right_two = [send_right(0, 2, 2, 1, c) for c in range(PARTS)]
     right_on = [send_right(1, 3, 2, 2, c) for c in range(PARTS)]
 
-    pl.semaphore_wait(barrier, n_wide - 1 + 2 * (shifts - 2))
-    for copy in right_one + [left_one]:
+    pl.semaphore_wait(barrier, 2 * (shifts - 1) + 2 * (shifts - 2))
+    early = right_one + [left_one]
+    late = [left_three] + right_two
+    for copy in early:
         copy.start()
+    say(0)
 
     for copy in gets:
         copy.wait()
@@ -179,77 +199,8 @@
     tot[...] = jnp.zeros_like(tot)
     low_w = lax.broadcasted_iota(jnp.int32, (EDGE, LANES), 1) < EDGE
 
-    def one_shift(i, carry):
-        s = jnp.where(i < 2, i, 2 + lax.rem(i + odd, 2))
-
-        @pl.when(i == 1)
-        def _():
-            for copy in right_one:
-                copy.wait_send()
-            for copy in [left_three] + right_two:
-                copy.start()
-            for c in range(PARTS):
-                got_right(1, c).wait()
-                right_on[c].start()
-            got_left(1).wait()
-
-            @pl.when(odd == 1)
-            def _():
-                left_on.start()
-
-        @pl.when(i == 2)
-        def _():
-            got_left(3).wait()
-
-            @pl.when(odd == 0)
-            def _():
-                left_on.start()
-                got_left(2).wait()
-
-        @pl.when((i == 3) & (odd == 1))
-        def _():
-            got_left(2).wait()
-
-        sel = wsel[s]
-        for q in range(tiles // 2):
-            a = jnp.dot(
-                sel, lbuf[s, :, q * 2 * LANES : (q + 1) * 2 * LANES], preferred_element_type=f32
-            )
-            hi = a.astype(bf16)
-            lo = (a - hi.astype(f32)).astype(bf16)
-            for h in range(2):
-                at = (2 * q + h) * nc
-                for r in range(nr):
-                    src = (slice(r * nc, (r + 1) * nc), slice(h * LANES, (h + 1) * LANES))
-                    both[at : at + nc, r * LANES : (r + 1) * LANES] = hi[src]
-                    both[half + at : half + at + nc, r * LANES : (r + 1) * LANES] = lo[src]
-
-        @pl.when(i > 1)
-        def _():
-            for c in range(PARTS):
-                got_right(s, c).wait()
-
-        for p in range(nr // 2):
-            pair = rbuf[s, p * EDGE : (p + 1) * EDGE, :].astype(f32)
-            turned = pltpu.roll(pair, EDGE, 1)
-            base = p * 4 * EDGE
-            wt[base : base + EDGE, :] = jnp.where(low_w, pair, 0.0).astype(bf16)
-            wt[base + EDGE : base + 2 * EDGE, :] = jnp.where(low_w, 0.0, turned).astype(bf16)
-            wt[base + 2 * EDGE : base + 3 * EDGE, :] = jnp.where(low_w, turned, 0.0).astype(bf16)
-            wt[base + 3 * EDGE : base + 4 * EDGE, :] = jnp.where(low_w, 0.0, pair).astype(bf16)
-        v = jnp.dot(both[...], wt[...], preferred_element_type=f32)
-        tot[...] += v[:half] + v[half:]
-        return carry
-
-    own_l.wait()
-    lax.fori_loop(0, shifts, one_shift, 0)
-
     eye = lax.broadcasted_iota(jnp.int32, (nc, nc), 0) == lax.broadcasted_iota(jnp.int32, (nc, nc), 1)
     keep = jnp.sum(jnp.where(eye, keep_ref[...].astype(f32), 0.0), axis=1, keepdims=True)
-    for t in range(tiles):
-        cols = slice(t * LANES, (t + 1) * LANES)
-        total = ebuf[:, cols] + tot[t * nc : (t + 1) * nc, :]
-        upd[:, cols] = ((1.5 * cbuf[:, cols] - 0.5 * total) * keep).astype(bf16)
     eye_w = lax.broadcasted_iota(jnp.int32, (n_wide, n_wide), 0) == lax.broadcasted_iota(
         jnp.int32, (n_wide, n_wide), 1
     )
@@ -259,27 +210,134 @@
         .astype(f32)
         .astype(bf16)
     )
-    for t in range(0, tiles, 4):
-        picked = jnp.dot(pick, upd[:, t * LANES : (t + 4) * LANES], preferred_element_type=f32)
-        for h in range(4):
-            rows[pl.ds(t + h, n_wide, stride=tiles), :] = picked[:, h * LANES : (h + 1) * LANES]
-
-    def send_block(k, carry):
-        d = lax.rem(w + k, n_wide)
-        outgoing[d] = rows[pl.ds(pl.multiple_of(d * tiles, tiles), tiles), :].astype(bf16)
-        pltpu.make_async_remote_copy(
-            src_ref=outgoing.at[d],
-            dst_ref=out_ref.at[w],
-            send_sem=asend.at[0],
-            recv_sem=arecv.at[0],
-            device_id={"wide": d},
-            device_id_type=MESH,
-        ).start()
+    keeps[...] = jnp.broadcast_to(keep, keeps.shape)
+    picks[...] = pick
+
+    group = tiles // SPLIT
+    deep = group * nc
+
+    def step(i, carry):
+        early_step = i < 2 * SPLIT
+        g = jnp.where(early_step, lax.rem(i, SPLIT), i // 2 - SPLIT)
+        s = jnp.where(early_step, i // SPLIT, 2 + lax.rem(i + odd, 2))
+        last = (i > 2 * SPLIT) & (lax.rem(i, 2) == 1)
+
+        @pl.when(i == SPLIT)
+        def _():
+            hear(0)
+            say(1)
+            for copy in right_one:
+                copy.wait_send()
+            for copy in late:
+                copy.start()
+            for c in range(PARTS):
+                got_right(1, c).wait()
+                right_on[c].start()
+            got_left(1).wait()
+
+            @pl.when(odd == 1)
+            def _():
+                left_on.start()
+
+            hear(1)
+            say(2)
+
+        @pl.when(i == 2 * SPLIT)
+        def _():
+            got_left(3).wait()
+
+            @pl.when(odd == 0)
+            def _():
+                left_on.start()
+                got_left(2).wait()
+
+        @pl.when((i == 2 * SPLIT + 1) & (odd == 1))
+        def _():
+            got_left(2).wait()
+
+        sel = wsel[s]
+        for q in range(group // 2):
+            cols = pl.ds(pl.multiple_of((g * group + 2 * q) * LANES, 2 * LANES), 2 * LANES)
+            a = jnp.dot(sel, lbuf[s, :, cols], preferred_element_type=f32)
+            hi = a.astype(bf16)
+            lo = (a - hi.astype(f32)).astype(bf16)
+            for h in range(2):
+                at = (2 * q + h) * nc
+                for r in range(nr):
+                    src = (slice(r * nc, (r + 1) * nc), slice(h * LANES, (h + 1) * LANES))
+                    both[at : at + nc, r * LANES : (r + 1) * LANES] = hi[src]
+                    both[deep + at : deep + at + nc, r * LANES : (r + 1) * LANES] = lo[src]
+
+        @pl.when((i >= 2 * SPLIT) & (i < 2 * SPLIT + 2))
+        def _():
+            for c in range(PARTS):
+                got_right(s, c).wait()
+
+        turn = lax.rem(s, 2)
+
+        @pl.when(g == 0)
+        def _():
+            for p in range(nr // 2):
+                pair = rbuf[s, p * EDGE : (p + 1) * EDGE, :].astype(f32)
+                turned = pltpu.roll(pair, EDGE, 1)
+                base = p * 4 * EDGE
+                wt[turn, base : base + EDGE, :] = jnp.where(low_w, pair, 0.0).astype(bf16)
+                wt[turn, base + EDGE : base + 2 * EDGE, :] = jnp.where(low_w, 0.0, turned).astype(bf16)
+                wt[turn, base + 2 * EDGE : base + 3 * EDGE, :] = jnp.where(low_w, turned, 0.0).astype(bf16)
+                wt[turn, base + 3 * EDGE : base + 4 * EDGE, :] = jnp.where(low_w, 0.0, pair).astype(bf16)
+
+        v = jnp.dot(both[...], wt[turn], preferred_element_type=f32)
+        part_rows = pl.ds(pl.multiple_of(g * deep, deep), deep)
+        tot[part_rows, :] += v[:deep] + v[deep:]
+
+        @pl.when(last)
+        def _():
+            @pl.when(g == 0)
+            def _():
+                hear(2)
+
+            mine = pl.ds(pl.multiple_of(g * group, group), group)
+            for t in range(group):
+                cols = pl.ds(pl.multiple_of((g * group + t) * LANES, LANES), LANES)
+                at = pl.ds(pl.multiple_of((g * group + t) * nc, nc), nc)
+                total = ebuf[:, cols] + tot[at, :]
+                upd[:, t * LANES : (t + 1) * LANES] = (
+                    (1.5 * cbuf[:, cols] - 0.5 * total) * keeps[...]
+                ).astype(bf16)
+            for t in range(0, group, 4):
+                picked = jnp.dot(
+                    picks[...], upd[:, t * LANES : (t + 4) * LANES], preferred_element_type=f32
+                )
+                for h in range(4):
+                    rows[pl.ds(t + h, n_wide, stride=group), :] = picked[
+                        :, h * LANES : (h + 1) * LANES
+                    ]
+
+            def to_send(d):
+                at = pl.ds(pl.multiple_of(d * group, group), group)
+                outgoing[d, mine] = rows[at, :].astype(bf16)
+
+            def send_block(j, carry):
+                d = lax.rem(w + j + 1, n_wide)
+                to_send(d)
+                pltpu.make_async_remote_copy(
+                    src_ref=outgoing.at[d, mine],
+                    dst_ref=out_ref.at[w, mine],
+                    send_sem=asend.at[0],
+                    recv_sem=arecv.at[0],
+                    device_id={"wide": d},
+                    device_id_type=MESH,
+                ).start()
+                return carry
+
+            lax.fori_loop(0, n_wide - 1, send_block, 0)
+            to_send(w)
+            pltpu.make_async_copy(outgoing.at[w, mine], out_ref.at[w, mine], arecv.at[0]).start()
+
         return carry
 
-    lax.fori_loop(1, n_wide, send_block, 0)
-    outgoing[w] = rows[pl.ds(pl.multiple_of(w * tiles, tiles), tiles), :].astype(bf16)
-    pltpu.make_async_copy(outgoing.at[w], out_ref.at[w], arecv.at[0]).start()
+    own_l.wait()
+    lax.fori_loop(0, shifts * SPLIT, step, 0)
 
     for copy in [left_one, left_three, left_on] + right_two + right_on:
         copy.wait_send()
@@ -327,11 +385,13 @@
             pltpu.VMEM((nr * tiles, LANES), f32),
             pltpu.VMEM((nr // 2 * EDGE, LANES), f32),
             pltpu.VMEM((shifts, nr * nc, nl), bf16),
-            pltpu.VMEM((2 * tiles * nc, nr * LANES), bf16),
-            pltpu.VMEM((nr * LANES, LANES), bf16),
+            pltpu.VMEM((2 * tiles // SPLIT * nc, nr * LANES), bf16),
+            pltpu.VMEM((2, nr * LANES, LANES), bf16),
             pltpu.VMEM((tiles * nc, LANES), f32),
-            pltpu.VMEM((nc, flat), bf16),
-            pltpu.VMEM((n_wide * tiles, LANES), f32),
+            pltpu.VMEM((nc, flat // SPLIT), bf16),
+            pltpu.VMEM((n_wide * tiles // SPLIT, LANES), f32),
+            pltpu.VMEM((nc, LANES), f32),
+            pltpu.VMEM((n_wide, nc), bf16),
             pltpu.VMEM((n_wide, tiles, LANES), bf16),
             dma((3,)),
             dma((shifts,)),
@@ -340,6 +400,7 @@
             dma((10,)),
             dma((1,)),
             dma((1,)),
+            pltpu.SemaphoreType.REGULAR((3,)),
         ],
         compiler_params=pltpu.CompilerParams(
             collective_id=0, has_side_effects=True, vmem_limit_bytes=VMEM_MIB * 1024 * 1024

time: 39.1 us -> 39.1 us (level)
  no operation moved by 1% of the time
where the time goes in v5:
time: 39.1 us; the launch traced here: 38.9 us
  Pallas kernels  38.1 us (97%)
  local copies, waits for them, and re-layouts  0.82 us (2%)
    pallas_call x1, Pallas kernels, per_device(): pl.pallas_call(functools.partial(kernel, n_wide, n_narrow, shifts), out_s...  38.1 us
    reshape x1, local copies, waits for them, and re-layouts, per_device(): return out.reshape(1, 1, n_wide, flat)  0.82 us

profile of v5, /device:TPU:1, one launch (start us, length us, event | category | flops | bytes accessed | tf_op | source)
XLA Modules:
  0.0 38.9 jit_solution(5392032286871042763)
XLA Ops:
  0.0 38.1 %shard_map.100 = bf16[32,32,128]{2,1,0:T(8,128)(2,1)S(1)} custom-call(bf16[24,4096]{1,0:T(8,128)(2,1)} %bitcast.12, bf16[16,4096]{1,0:T(8,128)(2,1)} %bitcast.13, f32[16,4096]{1,0:T(8,128)} %bitcast.10, f32[16,4096]{1,0:T(8,128)} %bitcast.11, s32[4,128]{1,0:T(4,128)} %bitcast.14, s32[4,128]{1,0:T(4,128)} %bitcast.15, s32[4,128]{1,0:T(4,128)} %bitcast.16, ...), custom_call_target="tpu_custom_call" | custom-call | flops 6442450944 | bytes 4194304 | tf_op jit(solution)/shard_map/pallas_call | solution.py:368
  38.1 0.8 %reshape.15 = bf16[1,1,32,4096]{3,2,1,0:T(8,128)(2,1)} reshape(bf16[32,32,128]{2,1,0:T(8,128)(2,1)S(1)} %shard_map.100) | data formatting | bytes 524288 | tf_op jit(solution)/shard_map/reshape | solution.py:412
